TPU v7x, 32 devices: a whole 2x2x4 slice. The times are simulated.
32 devices in a mesh: plots: 8 (over y, x, core), band: 4 (over z).
Axes of the slice: x: 2, y: 2, z: 4, core: 2. Of those that a mesh axis runs over, the one named last changes fastest.
Arguments:
- patches: bfloat16 [32, 1024, 768], P('plots', 'band'), may hold values from -6 to 6
- norm1_gain: float32 [768], replicated, may hold values from 0.1 to 1.9
- w_query: bfloat16 [768, 768], replicated, may hold values from -0.4375 to 0.4375
- w_key: bfloat16 [768, 768], replicated, may hold values from -0.21875 to 0.21875
- w_value: bfloat16 [768, 768], replicated, may hold values from -0.21875 to 0.21875
- w_out: bfloat16 [768, 768], replicated, may hold values from -0.875 to 0.875
- norm2_gain: float32 [768], replicated, may hold values from 0.1 to 1.9
- w_gate: bfloat16 [768, 2048], replicated, may hold values from -0.21875 to 0.21875
- w_up: bfloat16 [768, 2048], replicated, may hold values from -0.21875 to 0.21875
- w_down: bfloat16 [2048, 768], replicated, may hold values from -0.25 to 0.25
- out_grad: bfloat16 [32, 1024, 768], P('plots', 'band'), may hold values from -6 to 6
- plot_rows: int32 [32], P('plots'), may hold values from 8 to 16, as said below
- plot_cols: int32 [32], P('plots'), may hold values from 32 to 64
- global_index: int32 [32, 128], P('plots'), may hold values from 0 to 1023, as said below
Outputs:
- mixed_out: bfloat16 [32, 1024, 768], P('plots', 'band')
- patch_grad: bfloat16 [32, 1024, 768], P('plots', 'band')
- norm1_grad: float32 [768], replicated
- query_grad: float32 [768, 768], replicated
- key_grad: float32 [768, 768], replicated
- value_grad: float32 [768, 768], replicated
- out_proj_grad: float32 [768, 768], replicated
- norm2_grad: float32 [768], replicated
- gate_grad: float32 [768, 2048], replicated
- up_grad: float32 [768, 2048], replicated
- down_grad: float32 [2048, 768], replicated
Inputs may be any that keep to these rules, and one draw needn't show every extreme that they name: `plot_rows`: in each aligned group of 4 plots one plot has 16 rows and 64 columns. `global_index`: A plot's 128 indices are distinct valid slots of that plot.
All inputs are finite; a program needn't handle non-finite values.
Results may differ from a plain program's by a relative error of at most 0.017.
The roundings to bfloat16 on the way count: a program that leaves them out, or rounds other values in their place, can miss the bound.
Values may be sent and summed in bfloat16 or wider, within the bound.
No kernel may reach another device: no remote copies, remote signals or barrier semaphores. Data moves between devices by JAX's collectives and lax.ppermute only.
A program may use at most 256 MiB of HBM per device.

v0:
```python
import functools

import jax
import jax.numpy as jnp
from jax import lax
from jax.experimental import pallas as pl
from jax.experimental.pallas import tpu as pltpu
from jax.sharding import PartitionSpec as P

H = 12
HD = 64
COLS = 64
WIN = 2
TILE_ROWS = 2
PAIR = 2 * HD
BF = jnp.bfloat16
F32 = jnp.float32
LOG2E = 1.4426950408889634
SCALE2 = LOG2E * HD ** (-0.5)
SMALL = pl.CostEstimate(flops=10**10, bytes_accessed=1, transcendentals=0)

TINY = pl.CostEstimate(flops=1, bytes_accessed=1, transcendentals=0)
IN_VMEM = pl.BlockSpec(memory_space=pltpu.VMEM)
IN_SMEM = pl.BlockSpec(memory_space=pltpu.SMEM)


def dot_nt(a, b):
    return lax.dot_general(a, b, (((1,), (1,)), ((), ())), preferred_element_type=F32)


def dot_nn(a, b):
    return lax.dot_general(a, b, (((1,), (0,)), ((), ())), preferred_element_type=F32)


def dot_tn(a, b):
    return lax.dot_general(a, b, (((0,), (0,)), ((), ())), preferred_element_type=F32)


def tiles_of(rows):
    out = []
    for first in range(0, rows, TILE_ROWS):
        low = max(first - WIN, 0)
        high = min(first + TILE_ROWS + WIN, rows)
        out.append((first * COLS, low * COLS, high * COLS))
    return out


def fill_bias(bias_ref, limits_ref, tiles):
    rows_here = limits_ref[0]
    cols_here = limits_ref[1]
    span = TILE_ROWS * COLS
    for number, (query_lo, key_lo, key_hi) in enumerate(tiles):
        count = key_hi - key_lo
        shape = (count, 2 * span)
        key = lax.broadcasted_iota(jnp.int32, shape, 0) + key_lo
        query = lax.broadcasted_iota(jnp.int32, shape, 1) % span + query_lo
        key_row = key // COLS
        apart = key_row - query // COLS
        seen = (apart <= WIN) & (apart >= -WIN) & (key_row < rows_here) & (key % COLS < cols_here)
        bias_ref[number, :count, :] = jnp.where(seen, 0.0, -1e30).astype(F32)


def picker_rows(index_ref, slots):
    chosen = index_ref[:, 0:1]
    lanes = lax.broadcasted_iota(jnp.int32, (chosen.shape[0], slots), 1)
    return (lanes == chosen).astype(F32).astype(BF)


def two_heads(block, lane):
    none = jnp.zeros_like(block)
    return jnp.concatenate([jnp.where(lane < HD, block, none), jnp.where(lane < HD, none, block)])


def own_heads(sums, span):
    return jnp.transpose(jnp.concatenate([sums[:HD, :span], sums[HD:, span:]], axis=0))


def masks_kernel(limits_ref, index_ref, index_t_ref, bias_ref, pick_ref, pick_t_ref):
    slots = pick_ref.shape[1]
    fill_bias(bias_ref, limits_ref, tiles_of(slots // COLS))
    pick_ref[...] = picker_rows(index_ref, slots)
    down = lax.broadcasted_iota(jnp.int32, pick_t_ref.shape, 0)
    pick_t_ref[...] = (down == index_t_ref[0:1, :]).astype(F32).astype(BF)


def masks(limits, index, index_t, slots):
    count = index.shape[0]
    tall = (TILE_ROWS + 2 * WIN) * COLS
    tiles = slots // (TILE_ROWS * COLS)
    return pl.pallas_call(
        masks_kernel,
        in_specs=[IN_SMEM, IN_VMEM, IN_VMEM],
        out_specs=[IN_VMEM] * 3,
        out_shape=[
            jax.ShapeDtypeStruct((tiles, tall, 2 * TILE_ROWS * COLS), F32),
            jax.ShapeDtypeStruct((count, slots), BF),
            jax.ShapeDtypeStruct((slots, count), BF),
        ],
        compiler_params=pltpu.CompilerParams(vmem_limit_bytes=8 * 2**20),
        cost_estimate=SMALL,
        name="masks",
    )(limits, index, index_t)


def attend_kernel(bias_ref, pick_ref, q_ref, k_ref, v_ref, out_ref, lse_ref, value_t):
    slots = q_ref.shape[0]
    tiles = tiles_of(slots // COLS)
    span = TILE_ROWS * COLS
    global_keys = dot_nn(pick_ref[...], k_ref[...]).astype(BF)
    global_values_t = jnp.transpose(dot_nn(pick_ref[...], v_ref[...])).astype(BF)
    value_t[...] = jnp.transpose(v_ref[...].astype(F32)).astype(BF)
    lane = lax.broadcasted_iota(jnp.int32, (span, PAIR), 1)
    for number, (query_lo, key_lo, key_hi) in enumerate(tiles):
        count = key_hi - key_lo
        query = two_heads(q_ref[query_lo : query_lo + span, :], lane)
        window = dot_nt(k_ref[key_lo:key_hi, :], query) * SCALE2 + bias_ref[number, :count, :]
        wide = dot_nt(global_keys, query) * SCALE2
        highest = jnp.maximum(
            jnp.max(window, axis=0, keepdims=True), jnp.max(wide, axis=0, keepdims=True)
        )
        window = jnp.exp2(window - highest)
        wide = jnp.exp2(wide - highest)
        total = jnp.sum(window, axis=0, keepdims=True) + jnp.sum(wide, axis=0, keepdims=True)
        inverse = 1.0 / total
        sums = dot_nn(value_t[:, key_lo:key_hi], (window * inverse).astype(BF))
        sums = sums + dot_nn(global_values_t, (wide * inverse).astype(BF))
        lse_ref[0, number : number + 1, :] = highest + jnp.log2(total)
        out_ref[query_lo : query_lo + span, :] = own_heads(sums, span).astype(BF)


def attend_back_kernel(
    bias_ref,
    pick_ref,
    pick_t_ref,
    q_ref,
    k_ref,
    v_ref,
    g_ref,
    lse_ref,
    out_ref,
    key_t,
    dk_acc,
    dv_acc,
):
    slots = q_ref.shape[0]
    tiles = tiles_of(slots // COLS)
    span = TILE_ROWS * COLS
    globals_here = pick_ref.shape[0]
    global_keys_f = dot_nn(pick_ref[...], k_ref[...])
    global_keys = global_keys_f.astype(BF)
    global_keys_t = jnp.transpose(global_keys_f).astype(BF)
    global_values = dot_nn(pick_ref[...], v_ref[...]).astype(BF)
    key_t[...] = jnp.transpose(k_ref[...].astype(F32)).astype(BF)
    dk_acc[...] = jnp.zeros_like(dk_acc)
    dv_acc[...] = jnp.zeros_like(dv_acc)
    dk_global = jnp.zeros((globals_here, PAIR), F32)
    dv_global = jnp.zeros((globals_here, PAIR), F32)
    lane = lax.broadcasted_iota(jnp.int32, (span, PAIR), 1)
    for number, (query_lo, key_lo, key_hi) in enumerate(tiles):
        count = key_hi - key_lo
        query = two_heads(q_ref[query_lo : query_lo + span, :], lane)
        grad = two_heads(g_ref[query_lo : query_lo + span, :], lane)
        keys = k_ref[key_lo:key_hi, :]
        values = v_ref[key_lo:key_hi, :]
        lse = lse_ref[0, number : number + 1, :]
        window = jnp.exp2(dot_nt(keys, query) * SCALE2 + (bias_ref[number, :count, :] - lse))
        wide = jnp.exp2(dot_nt(global_keys, query) * SCALE2 - lse)
        window_g = dot_nt(values, grad)
        wide_g = dot_nt(global_values, grad)
        weighted = jnp.sum(window * window_g, axis=0, keepdims=True) + jnp.sum(
            wide * wide_g, axis=0, keepdims=True
        )
        window_s = (window * (window_g - weighted)).astype(BF)
        wide_s = (wide * (wide_g - weighted)).astype(BF)
        dv_acc[key_lo:key_hi, :] += dot_nn(window.astype(BF), grad)
        dk_acc[key_lo:key_hi, :] += dot_nn(window_s, query)
        dv_global += dot_nn(wide.astype(BF), grad)
        dk_global += dot_nn(wide_s, query)
        sums = dot_nn(key_t[:, key_lo:key_hi], window_s) + dot_nn(global_keys_t, wide_s)
        sums = own_heads(sums, span) * HD ** (-0.5)
        out_ref[0, query_lo : query_lo + span, :] = sums.astype(BF)

    def spread(part):
        high = part.astype(BF)
        rest = part - high.astype(F32)
        middle = rest.astype(BF)
        low = (rest - middle.astype(F32)).astype(BF)
        picks = pick_t_ref[...]
        return dot_nn(picks, high) + dot_nn(picks, middle) + dot_nn(picks, low)

    out_ref[1] = ((dk_acc[...] + spread(dk_global)) * HD ** (-0.5)).astype(BF)
    out_ref[2] = (dv_acc[...] + spread(dv_global)).astype(BF)


def attention(query, keys, values, bias, pick):
    slots, width = query.shape
    pairs = width // PAIR
    block = pl.BlockSpec((slots, PAIR), lambda p: (0, p))
    tiles = slots // (TILE_ROWS * COLS)
    return pl.pallas_call(
        attend_kernel,
        grid=(pairs,),
        in_specs=[IN_VMEM, IN_VMEM, block, block, block],
        out_specs=[block, pl.BlockSpec((1, tiles, 2 * TILE_ROWS * COLS), lambda p: (p, 0, 0))],
        out_shape=[
            jax.ShapeDtypeStruct((slots, width), BF),
            jax.ShapeDtypeStruct((pairs, tiles, 2 * TILE_ROWS * COLS), F32),
        ],
        scratch_shapes=[pltpu.VMEM((PAIR, slots), BF)],
        compiler_params=pltpu.CompilerParams(vmem_limit_bytes=10 * 2**20),
        cost_estimate=SMALL,
        name="attend",
    )(bias, pick, query, keys, values)


def attention_back(query, keys, values, grad, lse, bias, pick, pick_t, first, count):
    slots = query.shape[0]
    block = pl.BlockSpec((slots, PAIR), lambda p: (0, first + p))
    return pl.pallas_call(
        attend_back_kernel,
        grid=(count,),
        in_specs=[IN_VMEM] * 3
        + [block] * 4
        + [pl.BlockSpec((1, *lse.shape[1:]), lambda p: (first + p, 0, 0))],
        out_specs=pl.BlockSpec((3, slots, PAIR), lambda p: (0, 0, p)),
        out_shape=jax.ShapeDtypeStruct((3, slots, count * PAIR), BF),
        scratch_shapes=[
            pltpu.VMEM((PAIR, slots), BF),
            pltpu.VMEM((slots, PAIR), F32),
            pltpu.VMEM((slots, PAIR), F32),
        ],
        compiler_params=pltpu.CompilerParams(vmem_limit_bytes=12 * 2**20),
        cost_estimate=SMALL,
        name="attend_back",
    )(bias, pick, pick_t, query, keys, values, grad, lse)


def project(piece, gain, weights):
    hidden = rms_norm(piece.astype(F32), gain).astype(BF)
    return [hidden] + [dot_nn(hidden, weight[...]).astype(BF) for weight in weights]


def front(piece, gain, *weights):
    def kernel(piece, gain, *refs):
        for out, value in zip(refs[3:], project(piece[...], gain[...], refs[:3])):
            out[...] = value

    return small("front", kernel, [piece.shape] * 4, piece, gain, *weights, cost=SMALL)


def front_last(pieces, parts, gain, *weights):
    count, (rows, width) = len(pieces), pieces[0].shape

    def kernel(here, *refs):
        refs = list(refs)
        pieces = [refs.pop(0) for _ in range(count)]
        parts = [[refs.pop(0) for _ in range(4)] for _ in range(count - 1)]
        gain, weights, outs = refs[0], refs[1:4], refs[4:]
        for bit in range(count):
            place = pl.ds(pl.multiple_of((here[0] ^ bit) * rows, rows), rows)
            outs[0][place, :] = pieces[bit][...]
            if bit < count - 1:
                values = [part[...] for part in parts[bit]]
            else:
                values = project(pieces[bit][...], gain[...], weights)
            for out, value in zip(outs[1:], values):
                out[place, :] = value

    return small(
        "front_last",
        kernel,
        [(count * rows, width)] * 5,
        *pieces,
        *[array for part in parts for array in part],
        gain,
        *weights,
        scalars=[lax.axis_index("band")],
        cost=SMALL,
    )


def middle_kernel(x_ref, attended_ref, w_out, gain_ref, resid_ref, hidden_ref, hidden_t):
    resid = x_ref[...].astype(F32) + dot_nn(attended_ref[...], w_out[...])
    resid_ref[...] = resid
    hidden = rms_norm(resid, gain_ref[...])
    hidden_ref[...] = hidden.astype(BF)
    hidden_t[...] = jnp.transpose(hidden).astype(BF)


def middle(x, attended, w_out, gain):
    slots, width = x.shape
    rows = 256
    block = pl.BlockSpec((rows, width), lambda g: (g, 0))
    return pl.pallas_call(
        middle_kernel,
        grid=(slots // rows,),
        in_specs=[block, block, IN_VMEM, IN_VMEM],
        out_specs=[block, block, pl.BlockSpec((width, rows), lambda g: (0, g))],
        out_shape=[
            jax.ShapeDtypeStruct((slots, width), F32),
            jax.ShapeDtypeStruct((slots, width), BF),
            jax.ShapeDtypeStruct((width, slots), BF),
        ],
        compiler_params=pltpu.CompilerParams(vmem_limit_bytes=12 * 2**20),
        cost_estimate=SMALL,
        name="middle",
    )(x, attended, w_out, gain)


def turn_kernel(in_ref, out_ref):
    out_ref[...] = jnp.transpose(in_ref[...].astype(F32)).astype(BF)


def turn(matrix):
    rows, columns = matrix.shape
    wide = 256
    return pl.pallas_call(
        turn_kernel,
        grid=(columns // wide,),
        in_specs=[pl.BlockSpec((rows, wide), lambda g: (0, g))],
        out_specs=pl.BlockSpec((wide, rows), lambda g: (g, 0)),
        out_shape=jax.ShapeDtypeStruct((columns, rows), BF),
        compiler_params=pltpu.CompilerParams(vmem_limit_bytes=8 * 2**20),
        cost_estimate=SMALL,
        name="turn",
    )(matrix)


def weight_grad_kernel(groups, swapped, norms, place_ref, *refs):
    refs, out_ref = list(refs[:-1]), refs[-1]
    rows = out_ref.shape[1]
    half = 4 * rows
    start = pl.multiple_of(place_ref[0] * half, half)

    def store(sums, at):
        for block in range(4):
            spot = (block >> 1) | ((block & 1) << 1) if swapped else block
            part = sums[block * rows : (block + 1) * rows]
            out_ref[spot ^ place_ref[1], :, at : at + sums.shape[1]] = part

    at = 0
    for spans in groups:
        mine = refs.pop(0)[pl.ds(start, half), :]
        for span in spans:
            right = refs.pop(0)
            for number, first, count in span:
                for step in range(0, count, 512):
                    wide = min(512, count - step)
                    columns = right[number, :, first + step : first + step + wide]
                    store(dot_nn(mine, columns).astype(BF), at)
                    at += wide
    if norms:
        top = lax.broadcasted_iota(jnp.int32, (8, 128), 0) == 0
        lane = lax.broadcasted_iota(jnp.int32, (8, 128), 1)
        columns = pl.ds(pl.multiple_of(start, 128), half)
        sums = jnp.zeros((half, 128), F32)
        for number, norm in enumerate(refs):
            picks = jnp.where(top & (lane == number), 1.0, 0.0)
            sums = sums + dot_tn(norm[:, columns], picks)
        store(sums.astype(BF), at)


def weight_grad(place, groups, norms=(), *, spans, swapped=False):
    half = groups[0][0].shape[0] // 2
    inputs = [array for left, rights in groups for array in (left, *rights)]
    total = sum(count for group in spans for span in group for _, _, count in span)
    total += 128 if norms else 0
    inputs += list(norms)
    return pl.pallas_call(
        functools.partial(weight_grad_kernel, spans, swapped, bool(norms)),
        in_specs=[IN_SMEM] + [IN_VMEM] * len(inputs),
        out_specs=IN_VMEM,
        out_shape=jax.ShapeDtypeStruct((4, half // 4, total), BF),
        compiler_params=pltpu.CompilerParams(vmem_limit_bytes=8 * 2**20),
        cost_estimate=SMALL,
        name="weight_grad",
    )(place, *inputs)


def ffn_kernel(
    place_ref,
    hidden_ref,
    hidden_t,
    dy_ref,
    dy_t,
    gate_w,
    up_w,
    down_w,
    inner_ref,
    gate_ref,
    up_ref,
    near_ref,
    far_ref,
):
    rows = 256
    slope = (2.0 / 3.141592653589793) ** 0.5
    for start in range(0, hidden_ref.shape[0], rows):
        here = slice(start, start + rows)
        gate = dot_nn(hidden_ref[here, :], gate_w[...])
        up = dot_nn(hidden_ref[here, :], up_w[...])
        back = dot_nn(dy_ref[here, :], down_w[...])
        square = gate * gate
        share = 0.5 + 0.5 * jnp.tanh(gate * (slope + (0.044715 * slope) * square))
        active = gate * share
        inner_ref[here, :] = (active * up).astype(BF)
        up_ref[here, :] = (back * active).astype(BF)
        steep = share + (active - active * share) * (
            2.0 * slope + (6.0 * 0.044715 * slope) * square
        )
        gate_ref[here, :] = (back * up * steep).astype(BF)
    height = near_ref.shape[2]
    late = pl.program_id(0) >= pl.num_programs(0) // 2
    turned = (False, True, late)
    lefts, rights = (hidden_t, hidden_t, dy_t), (gate_ref, up_ref, inner_ref)
    for number, (left, right, swapped) in enumerate(zip(lefts, rights, turned)):
        sums = dot_nn(left[...], right[...]).astype(BF)
        for half in range(2):

            def put(target, half=half, sums=sums, number=number, swapped=swapped):
                for block in range(4):
                    straight = block ^ place_ref[1]
                    crossed = ((block >> 1) | ((block & 1) << 1)) ^ place_ref[2]
                    at = (4 * half + block) * height
                    spot = jnp.where(swapped, crossed, straight)
                    target[number, spot] = sums[at : at + height]

            pl.when(place_ref[0] == half)(functools.partial(put, near_ref))
            pl.when(place_ref[0] != half)(functools.partial(put, far_ref))


def ffn(place, hidden, hidden_t, dy, dy_t, w_gate, w_up, w_down_t):
    tokens, width = hidden.shape
    units = w_gate.shape[1]
    chunk = 512
    weight = pl.BlockSpec((width, chunk), lambda g: (0, g))
    wide = pl.BlockSpec((tokens, chunk), lambda g: (0, g))
    half = pl.BlockSpec((3, 4, width // 8, chunk), lambda g: (0, 0, 0, g))
    return pl.pallas_call(
        ffn_kernel,
        grid=(units // chunk,),
        in_specs=[IN_SMEM] + [IN_VMEM] * 4 + [weight] * 3,
        out_specs=[wide, wide, wide, half, half],
        out_shape=[jax.ShapeDtypeStruct((tokens, units), BF)] * 3
        + [jax.ShapeDtypeStruct((3, 4, width // 8, units), BF)] * 2,
        compiler_params=pltpu.CompilerParams(vmem_limit_bytes=32 * 2**20),
        cost_estimate=SMALL,
        name="ffn",
    )(place, hidden, hidden_t, dy, dy_t, w_gate, w_up, w_down_t)


def norm_back(values, gain, grad):
    inverse = lax.rsqrt(jnp.mean(values * values, axis=-1, keepdims=True) + 1e-06)
    scaled = values * inverse
    pulled = grad * gain
    shared = jnp.mean(scaled * pulled, axis=-1, keepdims=True)
    return inverse * (pulled - scaled * shared), jnp.sum(grad * scaled, axis=0, keepdims=True)


def patch_kernel(splits, *refs):
    parts, refs = refs[:splits], refs[splits:]
    x_ref, grad_ref, gain_ref, *weights, out_ref, norm_ref = refs
    grad = 0.0
    for number, weight in enumerate(weights):
        part = jnp.concatenate([ref[number] for ref in parts], axis=1)
        grad = grad + dot_nn(part, weight[...])
    pulled, gain = norm_back(x_ref[...].astype(F32), gain_ref[...], grad)
    out_ref[...] = (pulled + grad_ref[...]).astype(BF)

    @pl.when(pl.program_id(0) == 0)
    def _():
        norm_ref[...] = jnp.zeros_like(norm_ref)

    norm_ref[0:1, :] += gain


def patch_back(parts, x, grad, gain, w_query, w_key, w_value):
    tokens, width = x.shape
    rows = 512
    slim = pl.BlockSpec((rows, width), lambda g: (g, 0))
    part_specs = [pl.BlockSpec((3, rows, part.shape[2]), lambda g: (0, g, 0)) for part in parts]
    return pl.pallas_call(
        functools.partial(patch_kernel, len(parts)),
        grid=(tokens // rows,),
        in_specs=part_specs + [slim, slim] + [IN_VMEM] * 4,
        out_specs=[slim, pl.BlockSpec((8, width), lambda g: (0, 0))],
        out_shape=[
            jax.ShapeDtypeStruct((tokens, width), BF),
            jax.ShapeDtypeStruct((8, width), F32),
        ],
        compiler_params=pltpu.CompilerParams(vmem_limit_bytes=22 * 2**20),
        cost_estimate=SMALL,
        name="patch_back",
    )(*parts, x, grad, gain, w_query, w_key, w_value)


def assemble_kernel(recipe, place_ref, near_ref, far_ref, *outs):
    step = pl.program_id(0)
    for far, ref in enumerate((near_ref, far_ref)):

        @pl.when((step >= 4) == (far == 1))
        def _(ref=ref):
            for out_ref, pieces in zip(outs, recipe):
                at = 0
                for first, columns in pieces:
                    part = ref[0, :, first : first + columns]
                    out_ref[:, at : at + columns] = part.astype(F32)
                    at += columns


def assemble(place, near, far, recipe):
    rows = near.shape[1]
    block = (1, rows, near.shape[2])
    widths = [sum(columns for _, columns in pieces) for pieces in recipe]
    return pl.pallas_call(
        functools.partial(assemble_kernel, recipe),
        grid_spec=pltpu.PrefetchScalarGridSpec(
            num_scalar_prefetch=1,
            grid=(8,),
            in_specs=[
                pl.BlockSpec(block, lambda g, place: (jnp.minimum(g, 3), 0, 0)),
                pl.BlockSpec(block, lambda g, place: (jnp.maximum(g - 4, 0), 0, 0)),
            ],
            out_specs=[pl.BlockSpec((rows, w), lambda g, place: (g ^ place[2], 0)) for w in widths],
        ),
        out_shape=[jax.ShapeDtypeStruct((8 * rows, w), F32) for w in widths],
        compiler_params=pltpu.CompilerParams(vmem_limit_bytes=16 * 2**20),
        cost_estimate=SMALL,
        name="assemble",
    )(place, near, far)


def assemble_turned_kernel(place_ref, near_ref, far_ref, out_ref, rows_ref):
    height = near_ref.shape[1]
    for far, ref in enumerate((near_ref, far_ref)):
        for at in range(4):
            block = (4 * far + at) ^ place_ref[2]
            start = pl.multiple_of(block * height, height)
            rows_ref[pl.ds(start, height), :] = ref[at].astype(F32)
    out_ref[...] = jnp.transpose(rows_ref[...])


def assemble_turned(place, near, far, firsts, columns):
    rows = near.shape[1]
    chunk = 256
    half = columns // 2 // chunk
    one, two = (first // chunk for first in firsts)

    def where(g, place):
        return (0, 0, jnp.where(g < half, one + g, two + g - half))

    return pl.pallas_call(
        assemble_turned_kernel,
        grid_spec=pltpu.PrefetchScalarGridSpec(
            num_scalar_prefetch=1,
            grid=(2 * half,),
            in_specs=[pl.BlockSpec((4, rows, chunk), where)] * 2,
            out_specs=pl.BlockSpec((chunk, 8 * rows), lambda g, place: (g, 0)),
            scratch_shapes=[pltpu.VMEM((8 * rows, chunk), F32)],
        ),
        out_shape=jax.ShapeDtypeStruct((columns, 8 * rows), F32),
        compiler_params=pltpu.CompilerParams(vmem_limit_bytes=12 * 2**20),
        cost_estimate=SMALL,
        name="assemble_turned",
    )(place, near, far)


def small(name, kernel, shapes, *inputs, scalars=(), cost=TINY):
    many = [jax.ShapeDtypeStruct(shape, BF) for shape in shapes]
    scalars = [jnp.stack(scalars)] if scalars else []
    return pl.pallas_call(
        kernel,
        in_specs=[IN_SMEM] * len(scalars) + [IN_VMEM] * len(inputs),
        out_specs=[IN_VMEM] * len(many),
        out_shape=many,
        compiler_params=pltpu.CompilerParams(vmem_limit_bytes=8 * 2**20),
        cost_estimate=cost,
        name=name,
    )(*scalars, *inputs)


def add_low(left, right):
    return (left.astype(F32) + right.astype(F32)).astype(BF)


def halve(near, arrived):
    half = near.shape[0] // 2
    shape = (half, *near.shape[1:])

    def kernel(near, come, stays, leaves):
        for block in range(half):
            stays[block] = add_low(near[block], come[block])
            leaves[block] = add_low(near[half + block], come[half + block])

    return small("halve", kernel, [shape, shape], near, arrived)


def first_halves_kernel(near, come, one_stays, one_leaves, two_stays, two_leaves):
    step = pl.program_id(0)
    units = near.shape[3]
    half = units // 2
    for number, outs in enumerate(((one_stays, two_stays), (one_leaves, two_leaves))):

        @pl.when((step >= 2) == (number == 1))
        def _(outs=outs):
            last = add_low(near[2, 0], come[2, 0])
            for stream, out in enumerate(outs):
                out[0, :, :units] = add_low(near[stream, 0], come[stream, 0])
                out[0, :, units:] = last[:, stream * half : (stream + 1) * half]


def first_halves(near, come):
    _, blocks, rows, units = near.shape
    wide = units + units // 2
    stays = pl.BlockSpec((1, rows, wide), lambda g: (jnp.minimum(g, 1), 0, 0))
    leaves = pl.BlockSpec((1, rows, wide), lambda g: (jnp.maximum(g - 2, 0), 0, 0))
    block = pl.BlockSpec((3, 1, rows, units), lambda g: (0, g, 0, 0))
    one, one_go, two, two_go = pl.pallas_call(
        first_halves_kernel,
        grid=(blocks,),
        in_specs=[block, block],
        out_specs=[stays, leaves, stays, leaves],
        out_shape=[jax.ShapeDtypeStruct((2, rows, wide), BF)] * 4,
        compiler_params=pltpu.CompilerParams(vmem_limit_bytes=14 * 2**20),
        cost_estimate=SMALL,
        name="first_halves",
    )(near, come)
    return (one, one_go), (two, two_go)


def join(near, arrived):
    half = near.shape[0]

    def kernel(near, come, out):
        for block in range(half):
            out[block] = near[block]
            out[half + block] = come[block]

    return small("join", kernel, [(2 * half, *near.shape[1:])], near, arrived)[0]


def join_both(one, one_come, two, two_come):
    blocks, rows, wide = one.shape
    other = two.shape[2]

    def kernel(one, one_come, two, two_come, out):
        for number, (left, right) in enumerate(((one, two), (one_come, two_come))):
            for block in range(blocks):
                at = blocks * number + block
                out[at, :, :wide] = left[block]
                out[(at >> 1) | ((at & 1) << 1), :, wide:] = right[block]

    shape = (2 * blocks, rows, wide + other)
    return small("join_both", kernel, [shape], one, one_come, two, two_come)[0]


def apart(blocks):
    count = blocks.shape[0]

    def kernel(here, blocks, *outs):
        for bit, out in enumerate(outs):
            out[...] = blocks[here[0] ^ bit]

    return small(
        "apart", kernel, [blocks.shape[1:]] * count, blocks, scalars=[lax.axis_index("band")]
    )


def in_order(*pieces):
    count = len(pieces)

    def kernel(here, *refs):
        for bit in range(count):
            refs[count][here[0] ^ bit] = refs[bit][...]

    shape = (count, *pieces[0].shape)
    return small("in_order", kernel, [shape], *pieces, scalars=[lax.axis_index("band")])[0]


def bit_of(axis, bit):
    return (lax.axis_index(axis) // bit) % 2


def rows_apart(axis, bit):
    def step(*streams):
        height = streams[0].shape[1] // 2
        widths = [stream.shape[2] for stream in streams[::2]]
        shape = (height, sum(widths))

        def kernel(mine, *refs):
            ins, (stays, leaves) = refs[:-2], refs[-2:]
            for out, half in ((stays, mine[0]), (leaves, 1 - mine[0])):
                rows = pl.ds(pl.multiple_of(half * height, height), height)
                at = 0
                for near, come, wide in zip(ins[::2], ins[1::2], widths):
                    out[:, at : at + wide] = add_low(near[0, rows, :], come[0, rows, :])
                    at += wide

        return small(
            "rows_apart", kernel, [shape, shape], *streams, scalars=[bit_of(axis, bit)]
        )

    return step


def add_up(near, come):
    def kernel(near, come, out):
        out[...] = add_low(near[...], come[...])

    return small("add_up", kernel, [near.shape], near, come)[0]


def rows_join(axis, bit, widths):
    def step(near, come):
        height = near.shape[0]

        def kernel(mine, near, come, *outs):
            for piece, half in ((near, mine[0]), (come, 1 - mine[0])):
                rows = pl.ds(pl.multiple_of(half * height, height), height)
                at = 0
                for out, wide in zip(outs, widths):
                    out[0, rows, :] = piece[:, at : at + wide]
                    at += wide

        shapes = [(1, 2 * height, wide) for wide in widths]
        return small("rows_join", kernel, shapes, near, come, scalars=[bit_of(axis, bit)])

    return step


CORE, ACROSS, ALONG = 1, 2, 4


def flip(axis, bit):
    count = lax.axis_size(axis)
    return [(i, i ^ bit) for i in range(count)]


def swap(array, axis, bit):
    return lax.ppermute(array, axis, flip(axis, bit))


def take(array, number, axis=0):
    return lax.dynamic_index_in_dim(array, number, axis, keepdims=False)


def exchange(pieces):
    return pieces[:1] + tuple(swap(piece, "band", bit + 1) for bit, piece in enumerate(pieces[1:]))


def far_bits():
    plots = lax.axis_size("plots")
    band = lax.axis_size("band")
    bits = [("plots", 1 << n) for n in range(3, plots.bit_length() - 1)]
    return bits + [("band", 1 << n) for n in range(band.bit_length() - 1)]


class Line:
    def __init__(self):
        self.last = ()

    def __call__(self, step, *inputs):
        inputs, _ = lax.optimization_barrier((inputs, self.last))
        self.last = step(*inputs)
        return self.last


def side(axis, bit):
    def step(*streams):
        sums = [add_low(near[0], come[0]) for near, come in zip(streams[::2], streams[1::2])]
        return split_far(axis, bit)(jnp.concatenate(sums, 1))

    return step


def split_far(axis, bit):
    def step(matrix):
        halves = matrix.reshape(2, matrix.shape[0] // 2, matrix.shape[1])
        mine = bit_of(axis, bit)
        return take(halves, mine), take(halves, 1 - mine)

    return step


def join_far(axis, bit):
    def step(matrix, other):
        return jnp.where(
            bit_of(axis, bit) == 0,
            jnp.concatenate([matrix, other]),
            jnp.concatenate([other, matrix]),
        )

    return step


def travel(run, widths, *streams):
    far = far_bits()
    if len(far) == 2:
        first, second = far
        near, leaves = run(rows_apart(*first), *streams)
        come = swap(leaves, *first)
        yield
        near = run(add_up, near, come)
        come = swap(near, *second)
        yield
        near = run(add_up, near, come)
        come = swap(near, *first)
        yield
        return run(rows_join(*first, widths), near, come)
    near, leaves = run(side(*far[0]), *streams)
    come = swap(leaves, *far[0])
    yield
    for axis, bit in far[1:]:
        near, leaves = run(
            lambda near, come, far=(axis, bit): split_far(*far)(add_low(near, come)), near, come
        )
        come = swap(leaves, axis, bit)
        yield
    near = run(add_low, near, come)
    for axis, bit in far[::-1]:
        come = swap(near, axis, bit)
        yield
        near = run(join_far(axis, bit), near, come)
    cuts = [sum(widths[: n + 1]) for n in range(len(widths) - 1)]
    return run(lambda a: jnp.split(a[None], cuts, 2), near)


def rest_of(steps):
    while True:
        try:
            next(steps)
        except StopIteration as end:
            return end.value


def rms_norm(values, gain):
    inverse = lax.rsqrt(jnp.mean(values * values, axis=-1, keepdims=True) + 1e-06)
    return values * inverse * gain


def per_device(
    patches,
    norm1_gain,
    w_query,
    w_key,
    w_value,
    w_out,
    norm2_gain,
    w_gate,
    w_up,
    w_down,
    out_grad,
    plot_rows,
    plot_cols,
    global_index,
):
    width = patches.shape[2]
    here = lax.axis_index("band")
    run = Line()
    slots = patches.shape[0] * patches.shape[1]
    count = patches.shape[0]
    pieces = list(run(apart, patches))
    pieces[1:3] = [swap(piece, "band", bit + 1) for bit, piece in enumerate(pieces[1:3])]
    gain = norm1_gain[None]
    weights = w_query, w_key, w_value
    parts = [run(front, pieces[0], gain, *weights)]
    last = run(lambda *a: a, *pieces[3:])
    pieces[3:] = [swap(piece, "band", bit + 3) for bit, piece in enumerate(last)]
    limits = jnp.stack([take(plot_rows, here), take(plot_cols, here)])
    chosen = take(global_index, here)
    index = jnp.broadcast_to(chosen[:, None], (chosen.shape[0], 128))
    index_t = jnp.broadcast_to(chosen[None, :], (8, chosen.shape[0]))
    bias, pick, pick_t = run(functools.partial(masks, slots=slots), limits, index, index_t)
    w_down_t = run(turn, w_down)
    parts.append(run(front, pieces[1], gain, *weights))
    w_query_t, w_key_t, w_value_t = (run(turn, w) for w in weights)
    for piece in pieces[2:-1]:
        parts.append(run(front, piece, gain, *weights))
    dy_pieces = run(apart, out_grad)
    pieces = run(lambda *a: a, *pieces)
    dy_pieces = exchange(run(lambda *a: a, *dy_pieces))
    x_low, hidden, query, keys, values = run(front_last, pieces, parts, gain, *weights)

    me = lax.axis_index("plots")
    core, across, along = me % 2, (me // ACROSS) % 2, (me // ALONG) % 2
    square, square_t = 2 * across + along, 2 * along + across
    whole = 4 * core + square
    place_near = jnp.stack([core, square, whole])
    place_far = jnp.stack([1 - core, square, whole])
    place_near_t = jnp.stack([core, square_t, whole])
    place_far_t = jnp.stack([1 - core, square_t, whole])
    ff = w_gate.shape[1]

    attended, lse = run(attention, query, keys, values, bias, pick)
    resid, hidden2, hidden2_t = run(middle, x_low, attended, w_out, norm2_gain[None])
    w_gate_t, w_up_t, w_out_t = run(turn, w_gate), run(turn, w_up), run(turn, w_out)
    dy = run(in_order, *dy_pieces).reshape(slots, width)
    dy_t = run(turn, dy)
    place_ffn = jnp.stack([core, square, square_t])
    inner, grad_gate, grad_up, ffn_near, ffn_far = run(
        ffn, place_ffn, hidden2, hidden2_t, dy, dy_t, w_gate, w_up, w_down_t
    )
    core_swap = functools.partial(swap, axis="plots", bit=CORE)
    across_swap = functools.partial(swap, axis="plots", bit=ACROSS)
    along_swap = functools.partial(swap, axis="plots", bit=ALONG)
    far = far_bits()

    ffn_come = core_swap(ffn_far)
    mixed_out = run(
        lambda resid, inner, w: (resid + dot_nn(inner, w)).astype(BF), resid, inner, w_down
    )
    mixed_pieces = run(apart, mixed_out.reshape(patches.shape))
    (gate_near, gate_go), (up_near, up_go) = run(first_halves, ffn_near, ffn_come)
    gate_come, up_come = across_swap(gate_go), along_swap(up_go)
    mixed_pieces = exchange(run(lambda *a: a, *mixed_pieces))
    grad_hidden2 = run(
        lambda a, b, c, d: dot_nn(a, c) + dot_nn(b, d), grad_gate, grad_up, w_gate_t, w_up_t
    )

    def resid_back(resid, dy, gain, grad):
        pulled, norm2 = norm_back(resid, gain, grad)
        pulled = pulled + dy.astype(F32)
        return pulled, pulled.astype(BF), jnp.broadcast_to(norm2, (8, width))

    grad_resid, resid_low, norm2 = run(resid_back, resid, dy, norm2_gain, grad_hidden2)
    grad_attended = run(lambda a, w: dot_nn(a, w).astype(BF), resid_low, w_out_t)
    third = width // PAIR // 3

    def back(first):
        return run(
            functools.partial(attention_back, first=first, count=third),
            query,
            keys,
            values,
            grad_attended,
            lse,
            bias,
            pick,
            pick_t,
        )

    back_0 = back(0)
    gate_near, gate_go = run(halve, gate_near, gate_come)
    gate_come = along_swap(gate_go)
    up_near, up_go = run(halve, up_near, up_come)
    up_come = across_swap(up_go)
    back_1 = back(third)
    mixed_out = run(in_order, *mixed_pieces)
    attended_t = run(turn, attended)
    wide_ffn = ff + ff // 2
    ffn_steps = travel(run, [wide_ffn] * 2, gate_near, gate_come, up_near, up_come)
    next(ffn_steps)
    back_2 = back(2 * third)
    hidden_t = run(turn, hidden)
    next(ffn_steps)

    parts = [back_0, back_1, back_2]
    wide = third * PAIR
    half = wide // 2
    rest = width // 2
    out_right = resid_low[None]
    groups = [(hidden_t, parts), (attended_t, [out_right])]
    q_spans = [[[(0, 0, wide), (1, 0, half)]] * 3, [[(0, 0, rest)]]]
    v_spans = [[[(1, half, half), (2, 0, wide)]] * 3, [[(0, rest, width - rest)]]]
    q_grad = functools.partial(weight_grad, spans=q_spans)
    patch_grad, norm1 = run(
        patch_back, parts, x_low, grad_resid, norm1_gain[None], w_query_t, w_key_t, w_value_t
    )
    v_grad = functools.partial(weight_grad, spans=v_spans, swapped=True)
    norms = [norm1, norm2]
    pieces = list(run(apart, patch_grad.reshape(patches.shape)))
    q_come = core_swap(run(q_grad, place_far, groups))
    v_come = core_swap(run(v_grad, place_far_t, groups, norms))
    q_near = run(q_grad, place_near, groups)
    q_near, leaves = run(halve, q_near, q_come)
    q_come = across_swap(leaves)
    v_near = run(v_grad, place_near_t, groups, norms)
    v_near, leaves = run(halve, v_near, v_come)
    v_come = along_swap(leaves)
    next(ffn_steps)
    q_near, leaves = run(halve, q_near, q_come)
    q_come = along_swap(leaves)
    v_near, leaves = run(halve, v_near, v_come)
    v_come = across_swap(leaves)
    cut = 3 * (wide + half) + rest
    qkv_steps = travel(
        run, [cut, 3 * (wide + half) + width - rest + 128], q_near, q_come, v_near, v_come
    )
    next(qkv_steps)
    gate_all, up_all = rest_of(ffn_steps)
    gate_come, up_come = along_swap(gate_all), across_swap(up_all)
    next(qkv_steps)
    gate_all = run(join, gate_all, gate_come)
    gate_come = across_swap(gate_all)
    up_all = run(join, up_all, up_come)
    up_come = along_swap(up_all)
    next(qkv_steps)
    q_all, v_all = rest_of(qkv_steps)
    q_come, v_come = along_swap(q_all), across_swap(v_all)
    far_piece = swap(run(lambda a: a, pieces[2]), "band", 2)
    ffn_near = run(join_both, gate_all, gate_come, up_all, up_come)
    ffn_come = core_swap(ffn_near)
    q_all = run(join, q_all, q_come)
    q_come = across_swap(q_all)
    v_all = run(join, v_all, v_come)
    v_come = along_swap(v_all)
    gate, up = run(
        lambda near, far: assemble(place_near, near, far, [[(0, ff)], [(wide_ffn, ff)]]),
        ffn_near,
        ffn_come,
    )
    pieces[2] = run(lambda a: a, far_piece)
    qkv_near = run(join_both, q_all, q_come, v_all, v_come)
    qkv_come = core_swap(qkv_near)
    one, three = run(lambda *a: a, pieces[1], pieces[3])
    pieces[1], pieces[3] = swap(one, "band", 1), swap(three, "band", 3)
    down = run(
        lambda near, far: assemble_turned(place_near, near, far, (ff, wide_ffn + ff), ff),
        ffn_near,
        ffn_come,
    )
    recipe = [[], [], [], [(cut - rest, rest), (cut + 3 * (wide + half), width - rest)]]
    for number in range(3):
        at = number * (wide + half)
        recipe[0].append((at, wide))
        recipe[1] += [(at + wide, half), (cut + at, half)]
        recipe[2].append((cut + at + half, wide))
    recipe.append([(cut + 3 * (wide + half) + width - rest, 128)])
    q_out, k_out, v_out, out, gains = run(
        lambda near, far: assemble(place_near, near, far, recipe), qkv_near, qkv_come
    )
    patch_grad = run(in_order, *pieces)
    return (
        mixed_out,
        patch_grad,
        gains[:, 0],
        q_out,
        k_out,
        v_out,
        out,
        gains[:, 1],
        gate,
        up,
        down,
    )


def solution(mesh):
    rows = P("plots", "band", None)
    in_specs = (rows,) + (P(),) * 9 + (rows, P("plots"), P("plots"), P("plots", None))
    out_specs = (rows, rows) + (P(),) * 9
    return jax.shard_map(
        per_device, mesh=mesh, in_specs=in_specs, out_specs=out_specs, check_vma=False
    )
```

profile of v0, /device:TPU:0, one launch (start us, length us, event | category | flops | bytes accessed | tf_op | source)
XLA Modules:
  0.0 322.2 jit_solution(5481864010283802715)
XLA Ops:
  0.7 1.4 copy-done.4
  3.2 3.0 collective-permute-start
  6.2 2.6 collective-permute-start.1
  20.1 1.8 masks.1
  21.9 1.6 copy-done.30
  25.0 1.6 turn.10.down_w
  26.6 1.7 copy-done.28
  28.3 2.2 front.4
  35.6 2.3 front.5
  38.1 5.8 %collective-permute-start.3 = (bf16[256,768]{1,0:T(8,128)(2,1)S(1)}, bf16[256,768]{1,0:T(8,128)(2,1)S(1)}, u32[]{:S(2)}, u32[]{:S(2)}) collective-permute-start(bf16[256,768]{1,0:T(8,128)(2,1)S(1)} %get-tuple-element.373), channel_id=1, source_target_pairs={{0,1},{1,0},{2,3},{3,2},{4,5},{5,4},{6,7},{7,6},{8,9},{9,8},{10,11... | collective-permute-start | bytes 1179656 | tf_op jit(solution)/shard_map/ppermute | solution.py:739
  44.9 1.4 collective-permute-start.5
  46.4 2.8 front_last.1
  49.3 20.1 %attend.1 = (bf16[1024,768]{1,0:T(8,128)(2,1)S(1)}, f32[6,8,256]{2,1,0:T(8,128)S(1)}) custom-call(f32[8,384,256]{2,1,0:T(8,128)S(1)} %copy-done.31, bf16[128,1024]{1,0:T(8,128)(2,1)S(1)} %copy-done.60, bf16[1024,768]{1,0:T(8,128)(2,1)S(1)} %get-tuple-element.502.q_ref, bf16[1024,768]{1,0:T(8,128)(2,1)S(1)} %get-tuple-element.503.k_ref, ...), custom_call_target="tpu_custom_call" | custom-call | flops 10000000000 | bytes 1 | tf_op jit(solution)/shard_map/attend/pallas_call | solution.py:200
  69.5 2.9 middle.1
  72.5 1.9 turn.14
  74.4 1.6 copy-done.25
  76.0 1.9 turn.15
  77.9 1.7 copy-done.22
  83.8 28.7 %ffn.1 = (bf16[1024,2048]{1,0:T(8,128)(2,1)S(1)}, bf16[1024,2048]{1,0:T(8,128)(2,1)}, bf16[1024,2048]{1,0:T(8,128)(2,1)}, bf16[3,4,96,2048]{3,2,1,0:T(8,128)(2,1)}, bf16[3,4,96,2048]{3,2,1,0:T(8,128)(2,1)}) custom-call(s32[3]{0:T(128)S(1)} %pad_add_fusion.1.place_ref, bf16[1024,768]{1,0:T(8,128)(2,1)S(1)} %get-tuple-element.424.hidden_ref, ...), custom_call_target="tpu_custom_call" | custom-call | flops 10000000000 | bytes 1 | tf_op jit(solution)/shard_map/ffn/pallas_call | solution.py:438
  112.5 2.1 copy-done.24
  114.7 6.7 %add_convert_fusion = bf16[1024,768]{1,0:T(8,128)(2,1)S(1)} fusion(f32[1024,768]{1,0:T(8,128)S(1)} %get-tuple-element.458, bf16[1024,2048]{1,0:T(8,128)(2,1)} %copy-done.24, bf16[2048,768]{1,0:T(8,128)(2,1)} %in_ref), kind=kOutput, calls=%fused_computation.4 | convolution fusion | flops 3222798336 | bytes 12058624 | tf_op jit(solution)/shard_map/dot_general | solution.py:32
  122.8 3.9 %first_halves.1 = (bf16[2,96,3072]{2,1,0:T(8,128)(2,1)S(1)}, bf16[2,96,3072]{2,1,0:T(8,128)(2,1)S(1)}, bf16[2,96,3072]{2,1,0:T(8,128)(2,1)S(1)}, bf16[2,96,3072]{2,1,0:T(8,128)(2,1)S(1)}) custom-call(bf16[3,4,96,2048]{3,2,1,0:T(8,128)(2,1)S(1)} %copy-done.27, bf16[3,4,96,2048]{3,2,1,0:T(8,128)(2,1)} %collective-permute-done.6.come), custom_call_target="tpu_custom_call" | custom-call | flops 10000000000 | bytes 1 | tf_op jit(solution)/shard_map/first_halves/pallas_call | solution.py:617
  126.7 1.6 collective-permute-start.11
  128.3 1.5 collective-permute-start.10
  130.8 2.0 collective-permute-start.8
  132.8 1.4 collective-permute-start.9
  134.2 5.4 %fusion.1 = f32[1024,768]{1,0:T(8,128)S(1)} fusion(bf16[1024,2048]{1,0:T(8,128)(2,1)} %get-tuple-element.454, bf16[2048,768]{1,0:T(8,128)(2,1)S(1)} %copy-done.26), kind=kOutput, calls=%fused_computation.20 | convolution fusion | flops 3221225472 | bytes 10485760 | tf_op jit(solution)/shard_map/dot_general | solution.py:32
  139.6 3.4 %convolution_add_fusion = f32[1024,768]{1,0:T(8,128)S(1)} fusion(f32[1024,768]{1,0:T(8,128)S(1)} %fusion.1, bf16[1024,2048]{1,0:T(8,128)(2,1)S(1)} %copy-done.68, bf16[2048,768]{1,0:T(8,128)(2,1)S(1)} %copy-done.23), kind=kOutput, calls=%fused_computation.5 | convolution fusion | flops 3222011904 | bytes 13631488 | tf_op jit(solution)/shard_map/dot_general | solution.py:32
  146.5 1.4 convolution_convert_fusion.g_ref
  149.8 9.8 %attend_back.3.refs_0_.refs_1_ = bf16[3,1024,256]{2,1,0:T(8,128)(2,1)S(1)} custom-call(f32[8,384,256]{2,1,0:T(8,128)S(1)} %copy-done.32, bf16[128,1024]{1,0:T(8,128)(2,1)S(1)} %copy-done.61, bf16[1024,128]{1,0:T(8,128)(2,1)S(1)} %copy-done.63, bf16[1024,768]{1,0:T(8,128)(2,1)S(1)} %copy-done.36, bf16[1024,768]{1,0:T(8,128)(2,1)S(1)} %copy-done.38, ...), custom_call_target="tpu_custom_call" | custom-call | flops 10000000000 | bytes 1 | tf_op jit(solution)/shard_map/attend_back/pallas_call | solution.py:219
  161.4 10.0 %attend_back.4.refs_1_.refs_2_ = bf16[3,1024,256]{2,1,0:T(8,128)(2,1)S(1)} custom-call(f32[8,384,256]{2,1,0:T(8,128)S(1)} %copy-done.32, bf16[128,1024]{1,0:T(8,128)(2,1)S(1)} %copy-done.61, bf16[1024,128]{1,0:T(8,128)(2,1)S(1)} %copy-done.63, bf16[1024,768]{1,0:T(8,128)(2,1)S(1)} %copy-done.36, bf16[1024,768]{1,0:T(8,128)(2,1)S(1)} %copy-done.38, ...), custom_call_target="tpu_custom_call" | custom-call | flops 10000000000 | bytes 1 | tf_op jit(solution)/shard_map/attend_back/pallas_call | solution.py:219
  175.0 9.8 %attend_back.5.refs_2_.refs_3_ = bf16[3,1024,256]{2,1,0:T(8,128)(2,1)S(1)} custom-call(f32[8,384,256]{2,1,0:T(8,128)S(1)} %copy-done.32, bf16[128,1024]{1,0:T(8,128)(2,1)S(1)} %copy-done.61, bf16[1024,128]{1,0:T(8,128)(2,1)S(1)} %copy-done.63, bf16[1024,768]{1,0:T(8,128)(2,1)S(1)} %copy-done.36, bf16[1024,768]{1,0:T(8,128)(2,1)S(1)} %copy-done.38, ...), custom_call_target="tpu_custom_call" | custom-call | flops 10000000000 | bytes 1 | tf_op jit(solution)/shard_map/attend_back/pallas_call | solution.py:219
  185.7 2.3 collective-permute-done.14.come
  189.5 5.7 %patch_back.1 = (bf16[1024,768]{1,0:T(8,128)(2,1)S(1)}, f32[8,768]{1,0:T(8,128)S(1)}) custom-call(bf16[3,1024,256]{2,1,0:T(8,128)(2,1)S(1)} %attend_back.3.refs_0_.refs_1_, bf16[3,1024,256]{2,1,0:T(8,128)(2,1)S(1)} %attend_back.4.refs_1_.refs_2_, bf16[3,1024,256]{2,1,0:T(8,128)(2,1)S(1)} %attend_back.5.refs_2_.refs_3_, bf16[1024,768]{1,0:T(8,128)(2,1)S(1)} %copy-done.34, ...), custom_call_target="tpu_custom_call" | custom-call | flops 10000000000 | bytes 1 | tf_op jit(solution)/shard_map/patch_back/pallas_call | solution.py:481
  195.3 2.4 weight_grad.4
  197.7 2.4 weight_grad.5
  200.7 2.4 weight_grad.6.near
  203.4 2.4 weight_grad.7.near
  206.1 1.6 collective-permute-start.20
  207.7 1.4 collective-permute-start.16
  209.1 4.7 %collective-permute-done.17.come = bf16[48,6144]{1,0:T(8,128)(2,1)S(1)} collective-permute-done((bf16[48,6144]{1,0:T(8,128)(2,1)S(1)}, bf16[48,6144]{1,0:T(8,128)(2,1)S(1)}, u32[]{:S(2)}, u32[]{:S(2)}) %collective-permute-start.17) | collective-permute-done | bytes 589856 | tf_op jit(solution)/shard_map/ppermute | solution.py:739
  214.1 8.6 %collective-permute-done.16.come = bf16[2,96,1536]{2,1,0:T(8,128)(2,1)S(1)} collective-permute-done((bf16[2,96,1536]{2,1,0:T(8,128)(2,1)S(1)}, bf16[2,96,1536]{2,1,0:T(8,128)(2,1)S(1)}, u32[]{:S(2)}, u32[]{:S(2)}) %collective-permute-start.16) | collective-permute-done | bytes 589856 | tf_op jit(solution)/shard_map/ppermute | solution.py:739
  223.0 1.5 collective-permute-start.21
  225.6 6.3 %collective-permute-done.19.refs_1_ = bf16[1,96,1536]{2,1,0:T(8,128)(2,1)S(1)} collective-permute-done((bf16[1,96,1536]{2,1,0:T(8,128)(2,1)S(1)}, bf16[1,96,1536]{2,1,0:T(8,128)(2,1)S(1)}, u32[]{:S(2)}, u32[]{:S(2)}) %collective-permute-start.19) | collective-permute-done | bytes 294944 | tf_op jit(solution)/shard_map/ppermute | solution.py:739
  232.2 1.6 collective-permute-start.26
  234.6 1.7 collective-permute-start.22
  236.3 5.1 %collective-permute-done.22.come = bf16[48,3200]{1,0:T(8,128)(2,1)S(1)} collective-permute-done((bf16[48,3200]{1,0:T(8,128)(2,1)S(1)}, bf16[48,3200]{1,0:T(8,128)(2,1)S(1)}, u32[]{:S(2)}, u32[]{:S(2)}) %collective-permute-start.22) | collective-permute-done | bytes 307232 | tf_op jit(solution)/shard_map/ppermute | solution.py:739
  241.5 3.7 %collective-permute-done.26.come = bf16[1,96,3072]{2,1,0:T(8,128)(2,1)S(1)} collective-permute-done((bf16[1,96,3072]{2,1,0:T(8,128)(2,1)S(1)}, bf16[1,96,3072]{2,1,0:T(8,128)(2,1)S(1)}, u32[]{:S(2)}, u32[]{:S(2)}) %collective-permute-start.26) | collective-permute-done | bytes 589856 | tf_op jit(solution)/shard_map/ppermute | solution.py:739
  245.3 1.4 collective-permute-done.25.come
  248.3 1.7 collective-permute-start.24
  250.0 11.7 %collective-permute-done.24.come = bf16[48,3200]{1,0:T(8,128)(2,1)S(1)} collective-permute-done((bf16[48,3200]{1,0:T(8,128)(2,1)S(1)}, bf16[48,3200]{1,0:T(8,128)(2,1)S(1)}, u32[]{:S(2)}, u32[]{:S(2)}) %collective-permute-start.24) | collective-permute-done | bytes 307232 | tf_op jit(solution)/shard_map/ppermute | solution.py:739
  261.9 7.9 %collective-permute-done.27.come = bf16[48,3200]{1,0:T(8,128)(2,1)S(1)} collective-permute-done((bf16[48,3200]{1,0:T(8,128)(2,1)S(1)}, bf16[48,3200]{1,0:T(8,128)(2,1)S(1)}, u32[]{:S(2)}, u32[]{:S(2)}) %collective-permute-start.27) | collective-permute-done | bytes 307232 | tf_op jit(solution)/shard_map/ppermute | solution.py:739
  269.9 1.6 collective-permute-done.30.two_come
  275.0 1.7 collective-permute-start.34
  276.7 6.0 %collective-permute-done.28.come = bf16[1,96,1536]{2,1,0:T(8,128)(2,1)S(1)} collective-permute-done((bf16[1,96,1536]{2,1,0:T(8,128)(2,1)S(1)}, bf16[1,96,1536]{2,1,0:T(8,128)(2,1)S(1)}, u32[]{:S(2)}, u32[]{:S(2)}) %collective-permute-start.28) | collective-permute-done | bytes 294944 | tf_op jit(solution)/shard_map/ppermute | solution.py:739
  285.0 6.0 %assemble.2 = (f32[768,2048]{1,0:T(8,128)}, f32[768,2048]{1,0:T(8,128)}) custom-call(s32[3]{0:T(128)S(1)} %get-tuple-element.542.place_ref, bf16[4,96,6144]{2,1,0:T(8,128)(2,1)S(1)} %join_both.2.near_ref, bf16[4,96,6144]{2,1,0:T(8,128)(2,1)S(1)} %collective-permute-done.35.far_ref), custom_call_target="tpu_custom_call" | custom-call | flops 10000000000 | bytes 1 | tf_op jit(solution)/shard_map/assemble/pallas_call | solution.py:514
  291.0 4.3 %collective-permute-done.34.refs_2_ = bf16[256,768]{1,0:T(8,128)(2,1)S(1)} collective-permute-done((bf16[256,768]{1,0:T(8,128)(2,1)S(1)}, bf16[256,768]{1,0:T(8,128)(2,1)S(1)}, u32[]{:S(2)}, u32[]{:S(2)}) %collective-permute-start.34) | collective-permute-done | bytes 393248 | tf_op jit(solution)/shard_map/ppermute | solution.py:739
  295.3 2.2 collective-permute-done.31.one_come
  297.4 1.7 collective-permute-done.33.two_come
  299.3 1.8 collective-permute-start.36
  301.1 1.4 collective-permute-start.37
  302.5 6.0 %assemble_turned.1 = f32[2048,768]{1,0:T(8,128)} custom-call(s32[3]{0:T(128)S(1)} %get-tuple-element.542.place_ref, bf16[4,96,6144]{2,1,0:T(8,128)(2,1)S(1)} %join_both.2.near_ref, bf16[4,96,6144]{2,1,0:T(8,128)(2,1)S(1)} %collective-permute-done.35.far_ref), custom_call_target="tpu_custom_call" | custom-call | flops 10000000000 | bytes 1 | tf_op jit(solution)/shard_map/assemble_turned/pallas_call | solution.py:551
  308.5 5.3 %assemble.3 = (f32[768,768]{1,0:T(8,128)}, f32[768,768]{1,0:T(8,128)}, f32[768,768]{1,0:T(8,128)}, f32[768,768]{1,0:T(8,128)}, f32[768,128]{1,0:T(8,128)S(1)}) custom-call(s32[3]{0:T(128)S(1)} %get-tuple-element.542.place_ref, bf16[4,96,3200]{2,1,0:T(8,128)(2,1)S(1)} %join_both.3.near_ref, bf16[4,96,3200]{2,1,0:T(8,128)(2,1)S(1)} %collective-permute-done.38.far_ref), custom_call_target="tpu_custom_call" | custom-call | flops 10000000000 | bytes 1 | tf_op jit(solution)/shard_map/assemble/pallas_call | solution.py:514
  314.8 5.6 %collective-permute-done.37.refs_3_ = bf16[256,768]{1,0:T(8,128)(2,1)S(1)} collective-permute-done((bf16[256,768]{1,0:T(8,128)(2,1)S(1)}, bf16[256,768]{1,0:T(8,128)(2,1)S(1)}, u32[]{:S(2)}, u32[]{:S(2)}) %collective-permute-start.37) | collective-permute-done | bytes 393248 | tf_op jit(solution)/shard_map/ppermute | solution.py:739
  (231 shorter events, 53.8 us)
Async XLA Ops:
  0.6 18.0 %copy-start = (s32[4,128]{1,0:T(4,128)S(1)}, s32[4,128]{1,0:T(4,128)}, u32[]{:S(2)}) copy-start(s32[4,128]{1,0:T(4,128)} %param.27) | copy-start | bytes 6148
  3.2 11.3 %copy-start.18 = (bf16[256,768]{1,0:T(8,128)(2,1)}, bf16[256,768]{1,0:T(8,128)(2,1)S(1)}, u32[]{:S(2)}) copy-start(bf16[256,768]{1,0:T(8,128)(2,1)S(1)} %get-tuple-element.376.piece.refs_0_) | copy-start | bytes 1179652
  3.2 25.1 %collective-permute-start = (bf16[256,768]{1,0:T(8,128)(2,1)}, bf16[256,768]{1,0:T(8,128)(2,1)}, u32[]{:S(2)}, u32[]{:S(2)}) collective-permute-start(bf16[256,768]{1,0:T(8,128)(2,1)} %get-tuple-element.322), channel_id=1, source_target_pairs={{0,1},{1,0},{2,3},{3,2},{4,5},{5,4},{6,7},{7,6},{8,9},{9,8},{10,11... | collective-permute-start | bytes 1179656 | tf_op jit(solution)/shard_map/ppermute | solution.py:739
  6.2 29.4 %collective-permute-start.1 = (bf16[256,768]{1,0:T(8,128)(2,1)}, bf16[256,768]{1,0:T(8,128)(2,1)}, u32[]{:S(2)}, u32[]{:S(2)}) collective-permute-start(bf16[256,768]{1,0:T(8,128)(2,1)} %get-tuple-element.323), channel_id=1, source_target_pairs={{0,2},{1,3},{2,0},{3,1},{4,6},{5,7},{6,4},{7,5},{8,10},{9,11},{10,... | collective-permute-start | bytes 1179656 | tf_op jit(solution)/shard_map/ppermute | solution.py:739
  9.5 36.9 %copy-start.6 = (f32[1,768]{1,0:T(1,128)}, f32[1,768]{1,0:T(1,128)S(1)}, u32[]{:S(2)}) copy-start(f32[1,768]{1,0:T(1,128)S(1)} %broadcast_in_dim.14.gain.refs_16_.refs_5_) | copy-start | bytes 9220
  13.3 4.8 %copy-start.67 = (s32[4]{0:T(128)S(1)}, s32[4]{0:T(128)}, u32[]{:S(2)}) copy-start(s32[4]{0:T(128)} %param.26) | copy-start | bytes 52
  17.5 20.6 %collective-permute-start.2 = (bf16[256,768]{1,0:T(8,128)(2,1)}, bf16[256,768]{1,0:T(8,128)(2,1)}, u32[]{:S(2)}, u32[]{:S(2)}) collective-permute-start(bf16[256,768]{1,0:T(8,128)(2,1)} %get-tuple-element.334), channel_id=1, source_target_pairs={{0,3},{1,2},{2,1},{3,0},{4,7},{5,6},{6,5},{7,4},{8,11},{9,10},{10,... | collective-permute-start | bytes 1179656 | tf_op jit(solution)/shard_map/ppermute | solution.py:739
  20.1 4.9 %copy-start.10 = (bf16[2048,768]{1,0:T(8,128)(2,1)S(1)}, bf16[2048,768]{1,0:T(8,128)(2,1)}, u32[]{:S(2)}) copy-start(bf16[2048,768]{1,0:T(8,128)(2,1)} %in_ref) | copy-start | bytes 9437188
  35.6 10.8 %copy-start.19 = (bf16[256,768]{1,0:T(8,128)(2,1)S(1)}, bf16[256,768]{1,0:T(8,128)(2,1)}, u32[]{:S(2)}) copy-start(bf16[256,768]{1,0:T(8,128)(2,1)} %copy-done.18) | copy-start | bytes 1179652
  35.6 10.8 %copy-start.52 = (bf16[256,768]{1,0:T(8,128)(2,1)S(1)}, bf16[256,768]{1,0:T(8,128)(2,1)}, u32[]{:S(2)}) copy-start(bf16[256,768]{1,0:T(8,128)(2,1)} %copy-done.51) | copy-start | bytes 1179652
  35.6 10.8 %copy-start.54 = (bf16[256,768]{1,0:T(8,128)(2,1)S(1)}, bf16[256,768]{1,0:T(8,128)(2,1)}, u32[]{:S(2)}) copy-start(bf16[256,768]{1,0:T(8,128)(2,1)} %copy-done.53) | copy-start | bytes 1179652
  35.6 10.8 %copy-start.56 = (bf16[256,768]{1,0:T(8,128)(2,1)S(1)}, bf16[256,768]{1,0:T(8,128)(2,1)}, u32[]{:S(2)}) copy-start(bf16[256,768]{1,0:T(8,128)(2,1)} %copy-done.55) | copy-start | bytes 1179652
  35.6 10.8 %copy-start.58 = (bf16[256,768]{1,0:T(8,128)(2,1)S(1)}, bf16[256,768]{1,0:T(8,128)(2,1)}, u32[]{:S(2)}) copy-start(bf16[256,768]{1,0:T(8,128)(2,1)} %copy-done.57) | copy-start | bytes 1179652
  38.1 11.2 %copy-start.31 = (f32[8,384,256]{2,1,0:T(8,128)S(1)}, f32[8,384,256]{2,1,0:T(8,128)}, u32[]{:S(2)}) copy-start(f32[8,384,256]{2,1,0:T(8,128)} %copy-done.30) | copy-start | bytes 9437188
  38.1 11.2 %copy-start.60 = (bf16[128,1024]{1,0:T(8,128)(2,1)S(1)}, bf16[128,1024]{1,0:T(8,128)(2,1)}, u32[]{:S(2)}) copy-start(bf16[128,1024]{1,0:T(8,128)(2,1)} %copy-done.59) | copy-start | bytes 786436
  38.1 42.1 %collective-permute-start.3 = (bf16[256,768]{1,0:T(8,128)(2,1)S(1)}, bf16[256,768]{1,0:T(8,128)(2,1)S(1)}, u32[]{:S(2)}, u32[]{:S(2)}) collective-permute-start(bf16[256,768]{1,0:T(8,128)(2,1)S(1)} %get-tuple-element.373), channel_id=1, source_target_pairs={{0,1},{1,0},{2,3},{3,2},{4,5},{5,4},{6,7},{7,6},{8,9},{9,8},{10,11... | collective-permute-start | bytes 1179656 | tf_op jit(solution)/shard_map/ppermute | solution.py:739
  43.9 36.4 %collective-permute-start.4 = (bf16[256,768]{1,0:T(8,128)(2,1)S(1)}, bf16[256,768]{1,0:T(8,128)(2,1)S(1)}, u32[]{:S(2)}, u32[]{:S(2)}) collective-permute-start(bf16[256,768]{1,0:T(8,128)(2,1)S(1)} %get-tuple-element.374), channel_id=1, source_target_pairs={{0,2},{1,3},{2,0},{3,1},{4,6},{5,7},{6,4},{7,5},{8,10},{9,11},{10,... | collective-permute-start | bytes 1179656 | tf_op jit(solution)/shard_map/ppermute | solution.py:739
  44.9 35.3 %collective-permute-start.5 = (bf16[256,768]{1,0:T(8,128)(2,1)S(1)}, bf16[256,768]{1,0:T(8,128)(2,1)S(1)}, u32[]{:S(2)}, u32[]{:S(2)}) collective-permute-start(bf16[256,768]{1,0:T(8,128)(2,1)S(1)} %get-tuple-element.375), channel_id=1, source_target_pairs={{0,3},{1,2},{2,1},{3,0},{4,7},{5,6},{6,5},{7,4},{8,11},{9,10},{10,... | collective-permute-start | bytes 1179656 | tf_op jit(solution)/shard_map/ppermute | solution.py:739
  49.2 20.2 %copy-start.35 = (bf16[1024,768]{1,0:T(8,128)(2,1)}, bf16[1024,768]{1,0:T(8,128)(2,1)S(1)}, u32[]{:S(2)}) copy-start(bf16[1024,768]{1,0:T(8,128)(2,1)S(1)} %get-tuple-element.502.q_ref) | copy-start | bytes 4718596
  49.2 20.2 %copy-start.37 = (bf16[1024,768]{1,0:T(8,128)(2,1)}, bf16[1024,768]{1,0:T(8,128)(2,1)S(1)}, u32[]{:S(2)}) copy-start(bf16[1024,768]{1,0:T(8,128)(2,1)S(1)} %get-tuple-element.503.k_ref) | copy-start | bytes 4718596
  49.2 20.2 %copy-start.39 = (bf16[1024,768]{1,0:T(8,128)(2,1)}, bf16[1024,768]{1,0:T(8,128)(2,1)S(1)}, u32[]{:S(2)}) copy-start(bf16[1024,768]{1,0:T(8,128)(2,1)S(1)} %get-tuple-element.504.v_ref) | copy-start | bytes 4718596
  49.3 20.2 %copy-start.41 = (bf16[1024,768]{1,0:T(8,128)(2,1)}, bf16[1024,768]{1,0:T(8,128)(2,1)S(1)}, u32[]{:S(2)}) copy-start(bf16[1024,768]{1,0:T(8,128)(2,1)S(1)} %get-tuple-element.507.in_ref) | copy-start | bytes 4718596
  49.3 20.2 %copy-start.33 = (bf16[1024,768]{1,0:T(8,128)(2,1)}, bf16[1024,768]{1,0:T(8,128)(2,1)S(1)}, u32[]{:S(2)}) copy-start(bf16[1024,768]{1,0:T(8,128)(2,1)S(1)} %get-tuple-element.513.x_ref.refs_3_) | copy-start | bytes 4718596
  49.3 20.2 %copy-start.17 = (bf16[768,768]{1,0:T(8,128)(2,1)S(1)}, bf16[768,768]{1,0:T(8,128)(2,1)}, u32[]{:S(2)}) copy-start(bf16[768,768]{1,0:T(8,128)(2,1)} %in_ref.6) | copy-start | bytes 3538948
  114.6 8.3 %collective-permute-start.6 = (bf16[3,4,96,2048]{3,2,1,0:T(8,128)(2,1)}, bf16[3,4,96,2048]{3,2,1,0:T(8,128)(2,1)}, u32[]{:S(2)}, u32[]{:S(2)}) collective-permute-start(bf16[3,4,96,2048]{3,2,1,0:T(8,128)(2,1)} %get-tuple-element.435), channel_id=1, source_target_pairs={{0,4},{4,0},{8,12},{12,8},{16,20},{20,16},{24,28},{28,24},{1,5},{5... | collective-permute-start | bytes 14155784 | tf_op jit(solution)/shard_map/ppermute | solution.py:739
  114.7 8.1 %copy-start.27 = (bf16[3,4,96,2048]{3,2,1,0:T(8,128)(2,1)S(1)}, bf16[3,4,96,2048]{3,2,1,0:T(8,128)(2,1)}, u32[]{:S(2)}) copy-start(bf16[3,4,96,2048]{3,2,1,0:T(8,128)(2,1)} %get-tuple-element.444.near) | copy-start | bytes 14155780
  122.8 11.4 %copy-start.26 = (bf16[2048,768]{1,0:T(8,128)(2,1)S(1)}, bf16[2048,768]{1,0:T(8,128)(2,1)}, u32[]{:S(2)}) copy-start(bf16[2048,768]{1,0:T(8,128)(2,1)} %copy-done.25) | copy-start | bytes 9437188
  126.7 32.9 %collective-permute-start.11 = (bf16[2,96,3072]{2,1,0:T(8,128)(2,1)S(1)}, bf16[2,96,3072]{2,1,0:T(8,128)(2,1)S(1)}, u32[]{:S(2)}, u32[]{:S(2)}) collective-permute-start(bf16[2,96,3072]{2,1,0:T(8,128)(2,1)S(1)} %get-tuple-element.447), channel_id=1, source_target_pairs={{0,8},{4,12},{8,0},{12,4},{16,24},{20,28},{24,16},{28,20},{1,9},{5... | collective-permute-start | bytes 3538952 | tf_op jit(solution)/shard_map/ppermute | solution.py:739
  128.3 32.2 %collective-permute-start.10 = (bf16[2,96,3072]{2,1,0:T(8,128)(2,1)S(1)}, bf16[2,96,3072]{2,1,0:T(8,128)(2,1)S(1)}, u32[]{:S(2)}, u32[]{:S(2)}) collective-permute-start(bf16[2,96,3072]{2,1,0:T(8,128)(2,1)S(1)} %get-tuple-element.449), channel_id=1, source_target_pairs={{0,16},{4,20},{8,24},{12,28},{16,0},{20,4},{24,8},{28,12},{1,17},{... | collective-permute-start | bytes 3538952 | tf_op jit(solution)/shard_map/ppermute | solution.py:739
  129.8 9.8 %copy-start.23 = (bf16[2048,768]{1,0:T(8,128)(2,1)S(1)}, bf16[2048,768]{1,0:T(8,128)(2,1)}, u32[]{:S(2)}) copy-start(bf16[2048,768]{1,0:T(8,128)(2,1)} %copy-done.22) | copy-start | bytes 9437188
  129.8 9.8 %copy-start.68 = (bf16[1024,2048]{1,0:T(8,128)(2,1)S(1)}, bf16[1024,2048]{1,0:T(8,128)(2,1)}, u32[]{:S(2)}) copy-start(bf16[1024,2048]{1,0:T(8,128)(2,1)} %get-tuple-element.456) | copy-start | bytes 12582916
  129.8 41.6 %collective-permute-start.7 = (bf16[256,768]{1,0:T(8,128)(2,1)S(1)}, bf16[256,768]{1,0:T(8,128)(2,1)S(1)}, u32[]{:S(2)}, u32[]{:S(2)}) collective-permute-start(bf16[256,768]{1,0:T(8,128)(2,1)S(1)} %get-tuple-element.451), channel_id=1, source_target_pairs={{0,1},{1,0},{2,3},{3,2},{4,5},{5,4},{6,7},{7,6},{8,9},{9,8},{10,11... | collective-permute-start | bytes 1179656 | tf_op jit(solution)/shard_map/ppermute | solution.py:739
  130.8 40.6 %collective-permute-start.8 = (bf16[256,768]{1,0:T(8,128)(2,1)S(1)}, bf16[256,768]{1,0:T(8,128)(2,1)S(1)}, u32[]{:S(2)}, u32[]{:S(2)}) collective-permute-start(bf16[256,768]{1,0:T(8,128)(2,1)S(1)} %get-tuple-element.452), channel_id=1, source_target_pairs={{0,2},{1,3},{2,0},{3,1},{4,6},{5,7},{6,4},{7,5},{8,10},{9,11},{10,... | collective-permute-start | bytes 1179656 | tf_op jit(solution)/shard_map/ppermute | solution.py:739
  132.8 38.7 %collective-permute-start.9 = (bf16[256,768]{1,0:T(8,128)(2,1)S(1)}, bf16[256,768]{1,0:T(8,128)(2,1)S(1)}, u32[]{:S(2)}, u32[]{:S(2)}) collective-permute-start(bf16[256,768]{1,0:T(8,128)(2,1)S(1)} %get-tuple-element.453), channel_id=1, source_target_pairs={{0,3},{1,2},{2,1},{3,0},{4,7},{5,6},{6,5},{7,4},{8,11},{9,10},{10,... | collective-permute-start | bytes 1179656 | tf_op jit(solution)/shard_map/ppermute | solution.py:739
  159.9 14.6 %collective-permute-start.12 = (bf16[1,96,3072]{2,1,0:T(8,128)(2,1)S(1)}, bf16[1,96,3072]{2,1,0:T(8,128)(2,1)S(1)}, u32[]{:S(2)}, u32[]{:S(2)}) collective-permute-start(bf16[1,96,3072]{2,1,0:T(8,128)(2,1)S(1)} %get-tuple-element.475), channel_id=1, source_target_pairs={{0,16},{4,20},{8,24},{12,28},{16,0},{20,4},{24,8},{28,12},{1,17},{... | collective-permute-start | bytes 1769480 | tf_op jit(solution)/shard_map/ppermute | solution.py:739
  160.8 13.8 %collective-permute-start.13 = (bf16[1,96,3072]{2,1,0:T(8,128)(2,1)S(1)}, bf16[1,96,3072]{2,1,0:T(8,128)(2,1)S(1)}, u32[]{:S(2)}, u32[]{:S(2)}) collective-permute-start(bf16[1,96,3072]{2,1,0:T(8,128)(2,1)S(1)} %get-tuple-element.479), channel_id=1, source_target_pairs={{0,8},{4,12},{8,0},{12,4},{16,24},{20,28},{24,16},{28,20},{1,9},{5... | collective-permute-start | bytes 1769480 | tf_op jit(solution)/shard_map/ppermute | solution.py:739
  174.8 13.2 %collective-permute-start.14 = (bf16[48,6144]{1,0:T(8,128)(2,1)S(1)}, bf16[48,6144]{1,0:T(8,128)(2,1)S(1)}, u32[]{:S(2)}, u32[]{:S(2)}) collective-permute-start(bf16[48,6144]{1,0:T(8,128)(2,1)S(1)} %get-tuple-element.498), channel_id=1, source_target_pairs={{0,1},{1,0},{2,3},{3,2},{4,5},{5,4},{6,7},{7,6},{8,9},{9,8},{10,11... | collective-permute-start | bytes 1769480 | tf_op jit(solution)/shard_map/ppermute | solution.py:739
  175.0 9.9 %copy-start.42 = (bf16[1024,768]{1,0:T(8,128)(2,1)S(1)}, bf16[1024,768]{1,0:T(8,128)(2,1)}, u32[]{:S(2)}) copy-start(bf16[1024,768]{1,0:T(8,128)(2,1)} %copy-done.41) | copy-start | bytes 4718596
  184.8 4.6 %copy-start.7 = (f32[1,768]{1,0:T(1,128)S(1)}, f32[1,768]{1,0:T(1,128)}, u32[]{:S(2)}) copy-start(f32[1,768]{1,0:T(1,128)} %copy-done.6) | copy-start | bytes 9220
  188.1 25.7 %collective-permute-start.17 = (bf16[48,6144]{1,0:T(8,128)(2,1)S(1)}, bf16[48,6144]{1,0:T(8,128)(2,1)S(1)}, u32[]{:S(2)}, u32[]{:S(2)}) collective-permute-start(bf16[48,6144]{1,0:T(8,128)(2,1)S(1)} %add_up.4.near), channel_id=1, source_target_pairs={{0,2},{1,3},{2,0},{3,1},{4,6},{5,7},{6,4},{7,5},{8,10},{9,11},{10,... | collective-permute-start | bytes 1769480 | tf_op jit(solution)/shard_map/ppermute | solution.py:739
  197.6 5.4 %collective-permute-start.15 = (bf16[4,96,1536]{2,1,0:T(8,128)(2,1)S(1)}, bf16[4,96,1536]{2,1,0:T(8,128)(2,1)S(1)}, u32[]{:S(2)}, u32[]{:S(2)}) collective-permute-start(bf16[4,96,1536]{2,1,0:T(8,128)(2,1)S(1)} %weight_grad.4), channel_id=1, source_target_pairs={{0,4},{4,0},{8,12},{12,8},{16,20},{20,16},{24,28},{28,24},{1,5},{5... | collective-permute-start | bytes 3538952 | tf_op jit(solution)/shard_map/ppermute | solution.py:739
  200.2 5.6 %collective-permute-start.18 = (bf16[4,96,1664]{2,1,0:T(8,128)(2,1)S(1)}, bf16[4,96,1664]{2,1,0:T(8,128)(2,1)S(1)}, u32[]{:S(2)}, u32[]{:S(2)}) collective-permute-start(bf16[4,96,1664]{2,1,0:T(8,128)(2,1)S(1)} %weight_grad.5), channel_id=1, source_target_pairs={{0,4},{4,0},{8,12},{12,8},{16,20},{20,16},{24,28},{28,24},{1,5},{5... | collective-permute-start | bytes 3833864 | tf_op jit(solution)/shard_map/ppermute | solution.py:739
  206.1 16.7 %collective-permute-start.20 = (bf16[2,96,1664]{2,1,0:T(8,128)(2,1)S(1)}, bf16[2,96,1664]{2,1,0:T(8,128)(2,1)S(1)}, u32[]{:S(2)}, u32[]{:S(2)}) collective-permute-start(bf16[2,96,1664]{2,1,0:T(8,128)(2,1)S(1)} %get-tuple-element.565), channel_id=1, source_target_pairs={{0,16},{4,20},{8,24},{12,28},{16,0},{20,4},{24,8},{28,12},{1,17},{... | collective-permute-start | bytes 1916936 | tf_op jit(solution)/shard_map/ppermute | solution.py:739
  207.7 15.0 %collective-permute-start.16 = (bf16[2,96,1536]{2,1,0:T(8,128)(2,1)S(1)}, bf16[2,96,1536]{2,1,0:T(8,128)(2,1)S(1)}, u32[]{:S(2)}, u32[]{:S(2)}) collective-permute-start(bf16[2,96,1536]{2,1,0:T(8,128)(2,1)S(1)} %get-tuple-element.552), channel_id=1, source_target_pairs={{0,8},{4,12},{8,0},{12,4},{16,24},{20,28},{24,16},{28,20},{1,9},{5... | collective-permute-start | bytes 1769480 | tf_op jit(solution)/shard_map/ppermute | solution.py:739
  214.0 18.1 %collective-permute-start.23 = (bf16[48,6144]{1,0:T(8,128)(2,1)S(1)}, bf16[48,6144]{1,0:T(8,128)(2,1)S(1)}, u32[]{:S(2)}, u32[]{:S(2)}) collective-permute-start(bf16[48,6144]{1,0:T(8,128)(2,1)S(1)} %add_up.5.near), channel_id=1, source_target_pairs={{0,1},{1,0},{2,3},{3,2},{4,5},{5,4},{6,7},{7,6},{8,9},{9,8},{10,11... | collective-permute-start | bytes 1769480 | tf_op jit(solution)/shard_map/ppermute | solution.py:739
  223.0 9.0 %collective-permute-start.21 = (bf16[1,96,1664]{2,1,0:T(8,128)(2,1)S(1)}, bf16[1,96,1664]{2,1,0:T(8,128)(2,1)S(1)}, u32[]{:S(2)}, u32[]{:S(2)}) collective-permute-start(bf16[1,96,1664]{2,1,0:T(8,128)(2,1)S(1)} %get-tuple-element.575), channel_id=1, source_target_pairs={{0,8},{4,12},{8,0},{12,4},{16,24},{20,28},{24,16},{28,20},{1,9},{5... | collective-permute-start | bytes 958472 | tf_op jit(solution)/shard_map/ppermute | solution.py:739
  224.5 7.5 %collective-permute-start.19 = (bf16[1,96,1536]{2,1,0:T(8,128)(2,1)S(1)}, bf16[1,96,1536]{2,1,0:T(8,128)(2,1)S(1)}, u32[]{:S(2)}, u32[]{:S(2)}) collective-permute-start(bf16[1,96,1536]{2,1,0:T(8,128)(2,1)S(1)} %get-tuple-element.571), channel_id=1, source_target_pairs={{0,16},{4,20},{8,24},{12,28},{16,0},{20,4},{24,8},{28,12},{1,17},{... | collective-permute-start | bytes 884744 | tf_op jit(solution)/shard_map/ppermute | solution.py:739
  232.2 13.0 %collective-permute-start.26 = (bf16[1,96,3072]{2,1,0:T(8,128)(2,1)S(1)}, bf16[1,96,3072]{2,1,0:T(8,128)(2,1)S(1)}, u32[]{:S(2)}, u32[]{:S(2)}) collective-permute-start(bf16[1,96,3072]{2,1,0:T(8,128)(2,1)S(1)} %get-tuple-element.588.near), channel_id=1, source_target_pairs={{0,16},{4,20},{8,24},{12,28},{16,0},{20,4},{24,8},{28,12},{1,17},{... | collective-permute-start | bytes 1769480 | tf_op jit(solution)/shard_map/ppermute | solution.py:739
  233.8 13.0 %collective-permute-start.25 = (bf16[1,96,3072]{2,1,0:T(8,128)(2,1)S(1)}, bf16[1,96,3072]{2,1,0:T(8,128)(2,1)S(1)}, u32[]{:S(2)}, u32[]{:S(2)}) collective-permute-start(bf16[1,96,3072]{2,1,0:T(8,128)(2,1)S(1)} %get-tuple-element.590.near), channel_id=1, source_target_pairs={{0,8},{4,12},{8,0},{12,4},{16,24},{20,28},{24,16},{28,20},{1,9},{5... | collective-permute-start | bytes 1769480 | tf_op jit(solution)/shard_map/ppermute | solution.py:739
  234.6 6.9 %collective-permute-start.22 = (bf16[48,3200]{1,0:T(8,128)(2,1)S(1)}, bf16[48,3200]{1,0:T(8,128)(2,1)S(1)}, u32[]{:S(2)}, u32[]{:S(2)}) collective-permute-start(bf16[48,3200]{1,0:T(8,128)(2,1)S(1)} %get-tuple-element.581), channel_id=1, source_target_pairs={{0,1},{1,0},{2,3},{3,2},{4,5},{5,4},{6,7},{7,6},{8,9},{9,8},{10,11... | collective-permute-start | bytes 921608 | tf_op jit(solution)/shard_map/ppermute | solution.py:739
  246.8 24.7 %collective-permute-start.30 = (bf16[2,96,3072]{2,1,0:T(8,128)(2,1)S(1)}, bf16[2,96,3072]{2,1,0:T(8,128)(2,1)S(1)}, u32[]{:S(2)}, u32[]{:S(2)}) collective-permute-start(bf16[2,96,3072]{2,1,0:T(8,128)(2,1)S(1)} %join.5.two), channel_id=1, source_target_pairs={{0,16},{4,20},{8,24},{12,28},{16,0},{20,4},{24,8},{28,12},{1,17},{... | collective-permute-start | bytes 3538952 | tf_op jit(solution)/shard_map/ppermute | solution.py:739
  247.2 24.7 %collective-permute-start.29 = (bf16[2,96,3072]{2,1,0:T(8,128)(2,1)S(1)}, bf16[2,96,3072]{2,1,0:T(8,128)(2,1)S(1)}, u32[]{:S(2)}, u32[]{:S(2)}) collective-permute-start(bf16[2,96,3072]{2,1,0:T(8,128)(2,1)S(1)} %join.4.one), channel_id=1, source_target_pairs={{0,8},{4,12},{8,0},{12,4},{16,24},{20,28},{24,16},{28,20},{1,9},{5... | collective-permute-start | bytes 3538952 | tf_op jit(solution)/shard_map/ppermute | solution.py:739
  248.3 13.4 %collective-permute-start.24 = (bf16[48,3200]{1,0:T(8,128)(2,1)S(1)}, bf16[48,3200]{1,0:T(8,128)(2,1)S(1)}, u32[]{:S(2)}, u32[]{:S(2)}) collective-permute-start(bf16[48,3200]{1,0:T(8,128)(2,1)S(1)} %add_up.6.near), channel_id=1, source_target_pairs={{0,2},{1,3},{2,0},{3,1},{4,6},{5,7},{6,4},{7,5},{8,10},{9,11},{10,... | collective-permute-start | bytes 921608 | tf_op jit(solution)/shard_map/ppermute | solution.py:739
  261.8 8.0 %collective-permute-start.27 = (bf16[48,3200]{1,0:T(8,128)(2,1)S(1)}, bf16[48,3200]{1,0:T(8,128)(2,1)S(1)}, u32[]{:S(2)}, u32[]{:S(2)}) collective-permute-start(bf16[48,3200]{1,0:T(8,128)(2,1)S(1)} %add_up.7.near), channel_id=1, source_target_pairs={{0,1},{1,0},{2,3},{3,2},{4,5},{5,4},{6,7},{7,6},{8,9},{9,8},{10,11... | collective-permute-start | bytes 921608 | tf_op jit(solution)/shard_map/ppermute | solution.py:739
  272.3 12.7 %collective-permute-start.35 = (bf16[4,96,6144]{2,1,0:T(8,128)(2,1)S(1)}, bf16[4,96,6144]{2,1,0:T(8,128)(2,1)S(1)}, u32[]{:S(2)}, u32[]{:S(2)}) collective-permute-start(bf16[4,96,6144]{2,1,0:T(8,128)(2,1)S(1)} %join_both.2.near_ref), channel_id=1, source_target_pairs={{0,4},{4,0},{8,12},{12,8},{16,20},{20,16},{24,28},{28,24},{1,5},{5... | collective-permute-start | bytes 14155784 | tf_op jit(solution)/shard_map/ppermute | solution.py:739
  272.3 11.3 %collective-permute-start.32 = (bf16[1,96,1664]{2,1,0:T(8,128)(2,1)S(1)}, bf16[1,96,1664]{2,1,0:T(8,128)(2,1)S(1)}, u32[]{:S(2)}, u32[]{:S(2)}) collective-permute-start(bf16[1,96,1664]{2,1,0:T(8,128)(2,1)S(1)} %get-tuple-element.605.near), channel_id=1, source_target_pairs={{0,8},{4,12},{8,0},{12,4},{16,24},{20,28},{24,16},{28,20},{1,9},{5... | collective-permute-start | bytes 958472 | tf_op jit(solution)/shard_map/ppermute | solution.py:739
  273.7 9.1 %collective-permute-start.28 = (bf16[1,96,1536]{2,1,0:T(8,128)(2,1)S(1)}, bf16[1,96,1536]{2,1,0:T(8,128)(2,1)S(1)}, u32[]{:S(2)}, u32[]{:S(2)}) collective-permute-start(bf16[1,96,1536]{2,1,0:T(8,128)(2,1)S(1)} %get-tuple-element.603.near), channel_id=1, source_target_pairs={{0,16},{4,20},{8,24},{12,28},{16,0},{20,4},{24,8},{28,12},{1,17},{... | collective-permute-start | bytes 884744 | tf_op jit(solution)/shard_map/ppermute | solution.py:739
  275.0 20.2 %collective-permute-start.34 = (bf16[256,768]{1,0:T(8,128)(2,1)S(1)}, bf16[256,768]{1,0:T(8,128)(2,1)S(1)}, u32[]{:S(2)}, u32[]{:S(2)}) collective-permute-start(bf16[256,768]{1,0:T(8,128)(2,1)S(1)} %get-tuple-element.598), channel_id=1, source_target_pairs={{0,2},{1,3},{2,0},{3,1},{4,6},{5,7},{6,4},{7,5},{8,10},{9,11},{10,... | collective-permute-start | bytes 1179656 | tf_op jit(solution)/shard_map/ppermute | solution.py:739
  282.8 14.6 %collective-permute-start.31 = (bf16[2,96,1536]{2,1,0:T(8,128)(2,1)S(1)}, bf16[2,96,1536]{2,1,0:T(8,128)(2,1)S(1)}, u32[]{:S(2)}, u32[]{:S(2)}) collective-permute-start(bf16[2,96,1536]{2,1,0:T(8,128)(2,1)S(1)} %join.6.one), channel_id=1, source_target_pairs={{0,8},{4,12},{8,0},{12,4},{16,24},{20,28},{24,16},{28,20},{1,9},{5... | collective-permute-start | bytes 1769480 | tf_op jit(solution)/shard_map/ppermute | solution.py:739
  283.7 15.4 %collective-permute-start.33 = (bf16[2,96,1664]{2,1,0:T(8,128)(2,1)S(1)}, bf16[2,96,1664]{2,1,0:T(8,128)(2,1)S(1)}, u32[]{:S(2)}, u32[]{:S(2)}) collective-permute-start(bf16[2,96,1664]{2,1,0:T(8,128)(2,1)S(1)} %join.7.two), channel_id=1, source_target_pairs={{0,16},{4,20},{8,24},{12,28},{16,0},{20,4},{24,8},{28,12},{1,17},{... | collective-permute-start | bytes 1916936 | tf_op jit(solution)/shard_map/ppermute | solution.py:739
  299.3 9.3 %collective-permute-start.38 = (bf16[4,96,3200]{2,1,0:T(8,128)(2,1)S(1)}, bf16[4,96,3200]{2,1,0:T(8,128)(2,1)S(1)}, u32[]{:S(2)}, u32[]{:S(2)}) collective-permute-start(bf16[4,96,3200]{2,1,0:T(8,128)(2,1)S(1)} %join_both.3.near_ref), channel_id=1, source_target_pairs={{0,4},{4,0},{8,12},{12,8},{16,20},{20,16},{24,28},{28,24},{1,5},{5... | collective-permute-start | bytes 7372808 | tf_op jit(solution)/shard_map/ppermute | solution.py:739
  299.3 15.5 %collective-permute-start.36 = (bf16[256,768]{1,0:T(8,128)(2,1)S(1)}, bf16[256,768]{1,0:T(8,128)(2,1)S(1)}, u32[]{:S(2)}, u32[]{:S(2)}) collective-permute-start(bf16[256,768]{1,0:T(8,128)(2,1)S(1)} %get-tuple-element.616), channel_id=1, source_target_pairs={{0,1},{1,0},{2,3},{3,2},{4,5},{5,4},{6,7},{7,6},{8,9},{9,8},{10,11... | collective-permute-start | bytes 1179656 | tf_op jit(solution)/shard_map/ppermute | solution.py:739
  301.1 19.3 %collective-permute-start.37 = (bf16[256,768]{1,0:T(8,128)(2,1)S(1)}, bf16[256,768]{1,0:T(8,128)(2,1)S(1)}, u32[]{:S(2)}, u32[]{:S(2)}) collective-permute-start(bf16[256,768]{1,0:T(8,128)(2,1)S(1)} %get-tuple-element.617), channel_id=1, source_target_pairs={{0,3},{1,2},{2,1},{3,0},{4,7},{5,6},{6,5},{7,4},{8,11},{9,10},{10,... | collective-permute-start | bytes 1179656 | tf_op jit(solution)/shard_map/ppermute | solution.py:739
  308.5 13.2 %copy-start.1 = (s32[4,128]{1,0:T(4,128)S(1)}, s32[4,128]{1,0:T(4,128)}, u32[]{:S(2)}) copy-start(s32[4,128]{1,0:T(4,128)} %param.27) | copy-start | bytes 6148
  (44 other events, 96.2 us)
where the time goes:
time: 325 us; the launch traced here: 322 us
  Pallas kernels  146 us (45%)
  waiting for transfers between devices  75.3 us (23%)
  starting transfers between devices  47.6 us (15%)
  local copies, waits for them, and re-layouts  30.7 us (9%)
  matrix products  17 us (5%)
  other arithmetic  3.82 us (1%)
    ppermute x39, waiting for transfers between devices, swap(): return lax.ppermute(array, axis, flip(axis, bit))  75.3 us
    ppermute x39, starting transfers between devices, swap(): return lax.ppermute(array, axis, flip(axis, bit))  47.6 us
    pallas_call x3, Pallas kernels, attention_back(): pl.pallas_call(attend_back_kernel, grid=(count,), in_specs=[IN_VMEM] * 3...  29.7 us
    pallas_call x1, Pallas kernels, ffn(): pl.pallas_call(ffn_kernel, grid=(units // chunk,), in_specs=[IN_SMEM] + [...  28.7 us
    unnamed x138, local copies, waits for them, and re-layouts  27.8 us
    pallas_call x1, Pallas kernels, attention(): pl.pallas_call(attend_kernel, grid=(pairs,), in_specs=[IN_VMEM, IN_VMEM,...  20.1 us
    dot_general x4, matrix products, dot_nn(): lax.dot_general(a, b, (((1,), (0,)), ((), ())), preferred_element_type=F32)  17 us
    pallas_call x31, Pallas kernels, small(): pl.pallas_call(kernel, in_specs=[IN_SMEM] * len(scalars) + [IN_VMEM] * le...  15.6 us
  transfers between devices with their start and end apart: 39, of which 18 were waited for; matrix products, arithmetic and copies ran while one was open for 7% of the time, Pallas kernels for 34%

commit v1 on v0

--- a/solution.py
+++ b/solution.py
@@ -326,7 +326,7 @@
     )(matrix)
 
 
-def weight_grad_kernel(groups, swapped, norms, place_ref, *refs):
+def weight_grad_kernel(groups, swapped, place_ref, *refs):
     refs, out_ref = list(refs[:-1]), refs[-1]
     rows = out_ref.shape[1]
     half = 4 * rows
@@ -349,25 +349,14 @@
                     columns = right[number, :, first + step : first + step + wide]
                     store(dot_nn(mine, columns).astype(BF), at)
                     at += wide
-    if norms:
-        top = lax.broadcasted_iota(jnp.int32, (8, 128), 0) == 0
-        lane = lax.broadcasted_iota(jnp.int32, (8, 128), 1)
-        columns = pl.ds(pl.multiple_of(start, 128), half)
-        sums = jnp.zeros((half, 128), F32)
-        for number, norm in enumerate(refs):
-            picks = jnp.where(top & (lane == number), 1.0, 0.0)
-            sums = sums + dot_tn(norm[:, columns], picks)
-        store(sums.astype(BF), at)
-
-
-def weight_grad(place, groups, norms=(), *, spans, swapped=False):
+
+
+def weight_grad(place, groups, *, spans, swapped=False):
     half = groups[0][0].shape[0] // 2
     inputs = [array for left, rights in groups for array in (left, *rights)]
     total = sum(count for group in spans for span in group for _, _, count in span)
-    total += 128 if norms else 0
-    inputs += list(norms)
     return pl.pallas_call(
-        functools.partial(weight_grad_kernel, spans, swapped, bool(norms)),
+        functools.partial(weight_grad_kernel, spans, swapped),
         in_specs=[IN_SMEM] + [IN_VMEM] * len(inputs),
         out_specs=IN_VMEM,
         out_shape=jax.ShapeDtypeStruct((4, half // 4, total), BF),
@@ -442,7 +431,7 @@
         out_specs=[wide, wide, wide, half, half],
         out_shape=[jax.ShapeDtypeStruct((tokens, units), BF)] * 3
         + [jax.ShapeDtypeStruct((3, 4, width // 8, units), BF)] * 2,
-        compiler_params=pltpu.CompilerParams(vmem_limit_bytes=32 * 2**20),
+        compiler_params=pltpu.CompilerParams(vmem_limit_bytes=42 * 2**20),
         cost_estimate=SMALL,
         name="ffn",
     )(place, hidden, hidden_t, dy, dy_t, w_gate, w_up, w_down_t)
@@ -452,25 +441,18 @@
     inverse = lax.rsqrt(jnp.mean(values * values, axis=-1, keepdims=True) + 1e-06)
     scaled = values * inverse
     pulled = grad * gain
-    shared = jnp.mean(scaled * pulled, axis=-1, keepdims=True)
-    return inverse * (pulled - scaled * shared), jnp.sum(grad * scaled, axis=0, keepdims=True)
+    return inverse * (pulled - scaled * jnp.mean(scaled * pulled, axis=-1, keepdims=True))
 
 
 def patch_kernel(splits, *refs):
     parts, refs = refs[:splits], refs[splits:]
-    x_ref, grad_ref, gain_ref, *weights, out_ref, norm_ref = refs
+    x_ref, grad_ref, gain_ref, *weights, out_ref = refs
     grad = 0.0
     for number, weight in enumerate(weights):
         part = jnp.concatenate([ref[number] for ref in parts], axis=1)
         grad = grad + dot_nn(part, weight[...])
-    pulled, gain = norm_back(x_ref[...].astype(F32), gain_ref[...], grad)
+    pulled = norm_back(x_ref[...].astype(F32), gain_ref[...], grad)
     out_ref[...] = (pulled + grad_ref[...]).astype(BF)
-
-    @pl.when(pl.program_id(0) == 0)
-    def _():
-        norm_ref[...] = jnp.zeros_like(norm_ref)
-
-    norm_ref[0:1, :] += gain
 
 
 def patch_back(parts, x, grad, gain, w_query, w_key, w_value):
@@ -482,51 +464,56 @@
         functools.partial(patch_kernel, len(parts)),
         grid=(tokens // rows,),
         in_specs=part_specs + [slim, slim] + [IN_VMEM] * 4,
-        out_specs=[slim, pl.BlockSpec((8, width), lambda g: (0, 0))],
-        out_shape=[
-            jax.ShapeDtypeStruct((tokens, width), BF),
-            jax.ShapeDtypeStruct((8, width), F32),
-        ],
+        out_specs=slim,
+        out_shape=jax.ShapeDtypeStruct((tokens, width), BF),
         compiler_params=pltpu.CompilerParams(vmem_limit_bytes=22 * 2**20),
         cost_estimate=SMALL,
         name="patch_back",
     )(*parts, x, grad, gain, w_query, w_key, w_value)
 
 
-def assemble_kernel(recipe, place_ref, near_ref, far_ref, *outs):
+def assemble_kernel(recipe, scored, place_ref, near_ref, far_ref, *refs):
+    weights, outs, sums_ref = refs[:scored], refs[scored:-1], refs[-1]
     step = pl.program_id(0)
     for far, ref in enumerate((near_ref, far_ref)):
 
         @pl.when((step >= 4) == (far == 1))
         def _(ref=ref):
-            for out_ref, pieces in zip(outs, recipe):
+            sums = jnp.zeros((ref.shape[1], 1), F32)
+            for number, (out_ref, pieces) in enumerate(zip(outs, recipe)):
                 at = 0
                 for first, columns in pieces:
-                    part = ref[0, :, first : first + columns]
-                    out_ref[:, at : at + columns] = part.astype(F32)
+                    part = ref[0, :, first : first + columns].astype(F32)
+                    out_ref[:, at : at + columns] = part
+                    if number < scored:
+                        weight = weights[number][:, at : at + columns].astype(F32)
+                        sums = sums + jnp.sum(part * weight, axis=1, keepdims=True)
                     at += columns
-
-
-def assemble(place, near, far, recipe):
+            sums_ref[...] = jnp.broadcast_to(sums, sums_ref.shape)
+
+
+def assemble(place, near, far, weights, recipe):
     rows = near.shape[1]
     block = (1, rows, near.shape[2])
     widths = [sum(columns for _, columns in pieces) for pieces in recipe]
+    placed = [pl.BlockSpec((rows, w), lambda g, place: (g ^ place[2], 0)) for w in widths]
     return pl.pallas_call(
-        functools.partial(assemble_kernel, recipe),
+        functools.partial(assemble_kernel, recipe, len(weights)),
         grid_spec=pltpu.PrefetchScalarGridSpec(
             num_scalar_prefetch=1,
             grid=(8,),
             in_specs=[
                 pl.BlockSpec(block, lambda g, place: (jnp.minimum(g, 3), 0, 0)),
                 pl.BlockSpec(block, lambda g, place: (jnp.maximum(g - 4, 0), 0, 0)),
-            ],
-            out_specs=[pl.BlockSpec((rows, w), lambda g, place: (g ^ place[2], 0)) for w in widths],
+            ]
+            + placed[: len(weights)],
+            out_specs=placed + [pl.BlockSpec((rows, 128), lambda g, place: (g ^ place[2], 0))],
         ),
-        out_shape=[jax.ShapeDtypeStruct((8 * rows, w), F32) for w in widths],
-        compiler_params=pltpu.CompilerParams(vmem_limit_bytes=16 * 2**20),
+        out_shape=[jax.ShapeDtypeStruct((8 * rows, w), F32) for w in widths + [128]],
+        compiler_params=pltpu.CompilerParams(vmem_limit_bytes=18 * 2**20),
         cost_estimate=SMALL,
         name="assemble",
-    )(place, near, far)
+    )(place, near, far, *weights)
 
 
 def assemble_turned_kernel(place_ref, near_ref, far_ref, out_ref, rows_ref):
@@ -917,11 +904,10 @@
     )
 
     def resid_back(resid, dy, gain, grad):
-        pulled, norm2 = norm_back(resid, gain, grad)
-        pulled = pulled + dy.astype(F32)
-        return pulled, pulled.astype(BF), jnp.broadcast_to(norm2, (8, width))
-
-    grad_resid, resid_low, norm2 = run(resid_back, resid, dy, norm2_gain, grad_hidden2)
+        pulled = norm_back(resid, gain, grad) + dy.astype(F32)
+        return pulled, pulled.astype(BF)
+
+    grad_resid, resid_low = run(resid_back, resid, dy, norm2_gain, grad_hidden2)
     grad_attended = run(lambda a, w: dot_nn(a, w).astype(BF), resid_low, w_out_t)
     third = width // PAIR // 3
 
@@ -962,18 +948,17 @@
     q_spans = [[[(0, 0, wide), (1, 0, half)]] * 3, [[(0, 0, rest)]]]
     v_spans = [[[(1, half, half), (2, 0, wide)]] * 3, [[(0, rest, width - rest)]]]
     q_grad = functools.partial(weight_grad, spans=q_spans)
-    patch_grad, norm1 = run(
+    v_grad = functools.partial(weight_grad, spans=v_spans, swapped=True)
+    patch_grad = run(
         patch_back, parts, x_low, grad_resid, norm1_gain[None], w_query_t, w_key_t, w_value_t
     )
-    v_grad = functools.partial(weight_grad, spans=v_spans, swapped=True)
-    norms = [norm1, norm2]
     pieces = list(run(apart, patch_grad.reshape(patches.shape)))
     q_come = core_swap(run(q_grad, place_far, groups))
-    v_come = core_swap(run(v_grad, place_far_t, groups, norms))
+    v_come = core_swap(run(v_grad, place_far_t, groups))
     q_near = run(q_grad, place_near, groups)
     q_near, leaves = run(halve, q_near, q_come)
     q_come = across_swap(leaves)
-    v_near = run(v_grad, place_near_t, groups, norms)
+    v_near = run(v_grad, place_near_t, groups)
     v_near, leaves = run(halve, v_near, v_come)
     v_come = along_swap(leaves)
     next(ffn_steps)
@@ -983,7 +968,7 @@
     v_come = across_swap(leaves)
     cut = 3 * (wide + half) + rest
     qkv_steps = travel(
-        run, [cut, 3 * (wide + half) + width - rest + 128], q_near, q_come, v_near, v_come
+        run, [cut, 3 * (wide + half) + width - rest], q_near, q_come, v_near, v_come
     )
     next(qkv_steps)
     gate_all, up_all = rest_of(ffn_steps)
@@ -996,23 +981,25 @@
     next(qkv_steps)
     q_all, v_all = rest_of(qkv_steps)
     q_come, v_come = along_swap(q_all), across_swap(v_all)
-    far_piece = swap(run(lambda a: a, pieces[2]), "band", 2)
+    early = run(lambda *a: a, pieces[1], pieces[2])
+    early = [swap(piece, "band", bit + 1) for bit, piece in enumerate(early)]
     ffn_near = run(join_both, gate_all, gate_come, up_all, up_come)
     ffn_come = core_swap(ffn_near)
     q_all = run(join, q_all, q_come)
     q_come = across_swap(q_all)
     v_all = run(join, v_all, v_come)
     v_come = along_swap(v_all)
-    gate, up = run(
-        lambda near, far: assemble(place_near, near, far, [[(0, ff)], [(wide_ffn, ff)]]),
+    recipe_ffn = [[(0, ff)], [(wide_ffn, ff)]]
+    gate, up, sums2 = run(
+        lambda *arrays: assemble(place_near, *arrays, recipe_ffn),
         ffn_near,
         ffn_come,
-    )
-    pieces[2] = run(lambda a: a, far_piece)
+        [w_gate, w_up],
+    )
+    pieces[1:3] = run(lambda *a: a, *early)
     qkv_near = run(join_both, q_all, q_come, v_all, v_come)
     qkv_come = core_swap(qkv_near)
-    one, three = run(lambda *a: a, pieces[1], pieces[3])
-    pieces[1], pieces[3] = swap(one, "band", 1), swap(three, "band", 3)
+    pieces[3] = swap(run(lambda a: a, pieces[3]), "band", 3)
     down = run(
         lambda near, far: assemble_turned(place_near, near, far, (ff, wide_ffn + ff), ff),
         ffn_near,
@@ -1024,20 +1011,19 @@
         recipe[0].append((at, wide))
         recipe[1] += [(at + wide, half), (cut + at, half)]
         recipe[2].append((cut + at + half, wide))
-    recipe.append([(cut + 3 * (wide + half) + width - rest, 128)])
-    q_out, k_out, v_out, out, gains = run(
-        lambda near, far: assemble(place_near, near, far, recipe), qkv_near, qkv_come
+    q_out, k_out, v_out, out, sums1 = run(
+        lambda *arrays: assemble(place_near, *arrays, recipe), qkv_near, qkv_come, list(weights)
     )
     patch_grad = run(in_order, *pieces)
     return (
         mixed_out,
         patch_grad,
-        gains[:, 0],
+        sums1[:, 0] / norm1_gain,
         q_out,
         k_out,
         v_out,
         out,
-        gains[:, 1],
+        sums2[:, 0] / norm2_gain,
         gate,
         up,
         down,

time: 325 us -> 317 us (0.975)
  waiting for transfers between devices: 75.3 us -> 62.7 us
  starting transfers between devices: 47.6 us -> 52.5 us
  local copies, waits for them, and re-layouts: 30.7 us -> 27 us
    ppermute x39, waiting for transfers between devices: 75.3 us -> 62.7 us  [swap(): return lax.ppermute(array, axis, flip(axis, bit))]
    ppermute x39, starting transfers between devices: 47.6 us -> 52.5 us  [swap(): return lax.ppermute(array, axis, flip(axis, bit))]
    unnamed x138 -> x148, local copies, waits for them, and re-layouts: 27.8 us -> 24.7 us
  transfers between devices with their start and end apart: 39 -> 39, of which waited for: 18 -> 20; matrix products, arithmetic and copies ran while one was open for 7% -> 7% of each run, Pallas kernels for 34% -> 35%
where the time goes in v1:
time: 317 us; the launch traced here: 312 us
  Pallas kernels  148 us (47%)
  waiting for transfers between devices  62.7 us (20%)
  starting transfers between devices  52.5 us (17%)
  local copies, waits for them, and re-layouts  27 us (9%)
  matrix products  15 us (5%)
  other arithmetic  4.75 us (1%)
    ppermute x39, waiting for transfers between devices, swap(): return lax.ppermute(array, axis, flip(axis, bit))  62.7 us
    ppermute x39, starting transfers between devices, swap(): return lax.ppermute(array, axis, flip(axis, bit))  52.5 us
    pallas_call x3, Pallas kernels, attention_back(): pl.pallas_call(attend_back_kernel, grid=(count,), in_specs=[IN_VMEM] * 3...  29.9 us
    pallas_call x1, Pallas kernels, ffn(): pl.pallas_call(ffn_kernel, grid=(units // chunk,), in_specs=[IN_SMEM] + [...  28.9 us
    unnamed x148, local copies, waits for them, and re-layouts  24.7 us
    pallas_call x1, Pallas kernels, attention(): pl.pallas_call(attend_kernel, grid=(pairs,), in_specs=[IN_VMEM, IN_VMEM,...  20.1 us
    pallas_call x31, Pallas kernels, small(): pl.pallas_call(kernel, in_specs=[IN_SMEM] * len(scalars) + [IN_VMEM] * le...  15.5 us
    dot_general x4, matrix products, dot_nn(): lax.dot_general(a, b, (((1,), (0,)), ((), ())), preferred_element_type=F32)  15 us
  transfers between devices with their start and end apart: 39, of which 20 were waited for; matrix products, arithmetic and copies ran while one was open for 7% of the time, Pallas kernels for 35%

profile of v1, /device:TPU:0, one launch (start us, length us, event | category | flops | bytes accessed | tf_op | source)
XLA Modules:
  0.0 311.8 jit_solution(4969355166304012913)
XLA Ops:
  0.7 1.4 copy-done.4
  3.2 3.0 collective-permute-start
  6.2 2.6 collective-permute-start.1
  18.6 1.4 pad_add_fusion.limits_ref
  20.1 1.8 masks.1
  21.9 1.6 copy-done.33
  25.0 1.5 turn.10.down_w
  26.4 1.7 copy-done.32
  28.2 2.2 front.4
  34.9 2.3 front.5
  37.4 6.4 %collective-permute-start.3 = (bf16[256,768]{1,0:T(8,128)(2,1)S(1)}, bf16[256,768]{1,0:T(8,128)(2,1)S(1)}, u32[]{:S(2)}, u32[]{:S(2)}) collective-permute-start(bf16[256,768]{1,0:T(8,128)(2,1)S(1)} %get-tuple-element.374), channel_id=1, source_target_pairs={{0,1},{1,0},{2,3},{3,2},{4,5},{5,4},{6,7},{7,6},{8,9},{9,8},{10,11... | collective-permute-start | bytes 1179656 | tf_op jit(solution)/shard_map/ppermute | solution.py:726
  44.9 1.4 collective-permute-start.5
  46.4 2.8 front_last.1
  50.4 20.1 %attend.1 = (bf16[1024,768]{1,0:T(8,128)(2,1)S(1)}, f32[6,8,256]{2,1,0:T(8,128)S(1)}) custom-call(f32[8,384,256]{2,1,0:T(8,128)S(1)} %copy-done.34, bf16[128,1024]{1,0:T(8,128)(2,1)S(1)} %copy-done.63, bf16[1024,768]{1,0:T(8,128)(2,1)S(1)} %get-tuple-element.503.q_ref, bf16[1024,768]{1,0:T(8,128)(2,1)S(1)} %get-tuple-element.504.k_ref, ...), custom_call_target="tpu_custom_call" | custom-call | flops 10000000000 | bytes 1 | tf_op jit(solution)/shard_map/attend/pallas_call | solution.py:200
  70.6 2.9 middle.1
  73.6 1.9 turn.14
  75.5 1.7 copy-done.29
  77.2 1.9 turn.15
  83.0 28.9 %ffn.1 = (bf16[1024,2048]{1,0:T(8,128)(2,1)}, bf16[1024,2048]{1,0:T(8,128)(2,1)}, bf16[1024,2048]{1,0:T(8,128)(2,1)}, bf16[3,4,96,2048]{3,2,1,0:T(8,128)(2,1)}, bf16[3,4,96,2048]{3,2,1,0:T(8,128)(2,1)}) custom-call(s32[3]{0:T(128)S(1)} %pad_add_fusion.1.place_ref, bf16[1024,768]{1,0:T(8,128)(2,1)S(1)} %get-tuple-element.425.hidden_ref, ...), custom_call_target="tpu_custom_call" | custom-call | flops 10000000000 | bytes 1 | tf_op jit(solution)/shard_map/ffn/pallas_call | solution.py:427
  112.1 6.7 %add_convert_fusion = bf16[1024,768]{1,0:T(8,128)(2,1)S(1)} fusion(f32[1024,768]{1,0:T(8,128)S(1)} %get-tuple-element.459, bf16[1024,2048]{1,0:T(8,128)(2,1)} %get-tuple-element.438, bf16[2048,768]{1,0:T(8,128)(2,1)} %in_ref), kind=kOutput, calls=%fused_computation.3 | convolution fusion | flops 3222798336 | bytes 12058624 | tf_op jit(solution)/shard_map/dot_general | solution.py:32
  120.2 4.9 %first_halves.1 = (bf16[2,96,3072]{2,1,0:T(8,128)(2,1)S(1)}, bf16[2,96,3072]{2,1,0:T(8,128)(2,1)S(1)}, bf16[2,96,3072]{2,1,0:T(8,128)(2,1)S(1)}, bf16[2,96,3072]{2,1,0:T(8,128)(2,1)S(1)}) custom-call(bf16[3,4,96,2048]{3,2,1,0:T(8,128)(2,1)S(1)} %copy-done.31, bf16[3,4,96,2048]{3,2,1,0:T(8,128)(2,1)} %collective-permute-done.6.come), custom_call_target="tpu_custom_call" | custom-call | flops 10000000000 | bytes 1 | tf_op jit(solution)/shard_map/first_halves/pallas_call | solution.py:604
  125.2 1.6 collective-permute-start.11
  126.7 1.5 collective-permute-start.10
  129.3 2.0 collective-permute-start.8
  131.2 1.4 collective-permute-start.9
  132.6 3.4 %fusion.1 = f32[1024,768]{1,0:T(8,128)S(1)} fusion(bf16[1024,2048]{1,0:T(8,128)(2,1)S(1)} %copy-done.73, bf16[2048,768]{1,0:T(8,128)(2,1)S(1)} %copy-done.30), kind=kOutput, calls=%fused_computation.19 | convolution fusion | flops 3221225472 | bytes 10485760 | tf_op jit(solution)/shard_map/dot_general | solution.py:32
  136.1 3.4 %convolution_add_fusion = f32[1024,768]{1,0:T(8,128)S(1)} fusion(f32[1024,768]{1,0:T(8,128)S(1)} %fusion.1, bf16[1024,2048]{1,0:T(8,128)(2,1)S(1)} %copy-done.72, bf16[2048,768]{1,0:T(8,128)(2,1)S(1)} %copy-done.28), kind=kOutput, calls=%fused_computation.4 | convolution fusion | flops 3222011904 | bytes 13631488 | tf_op jit(solution)/shard_map/dot_general | solution.py:32
  142.9 1.4 convolution_convert_fusion.g_ref
  146.2 10.0 %attend_back.3.refs_0_.refs_1_ = bf16[3,1024,256]{2,1,0:T(8,128)(2,1)S(1)} custom-call(f32[8,384,256]{2,1,0:T(8,128)S(1)} %copy-done.35, bf16[128,1024]{1,0:T(8,128)(2,1)S(1)} %copy-done.64, bf16[1024,128]{1,0:T(8,128)(2,1)S(1)} %copy-done.66, bf16[1024,768]{1,0:T(8,128)(2,1)S(1)} %copy-done.39, bf16[1024,768]{1,0:T(8,128)(2,1)S(1)} %copy-done.41, ...), custom_call_target="tpu_custom_call" | custom-call | flops 10000000000 | bytes 1 | tf_op jit(solution)/shard_map/attend_back/pallas_call | solution.py:219
  158.0 9.8 %attend_back.4.refs_1_.refs_2_ = bf16[3,1024,256]{2,1,0:T(8,128)(2,1)S(1)} custom-call(f32[8,384,256]{2,1,0:T(8,128)S(1)} %copy-done.35, bf16[128,1024]{1,0:T(8,128)(2,1)S(1)} %copy-done.64, bf16[1024,128]{1,0:T(8,128)(2,1)S(1)} %copy-done.66, bf16[1024,768]{1,0:T(8,128)(2,1)S(1)} %copy-done.39, bf16[1024,768]{1,0:T(8,128)(2,1)S(1)} %copy-done.41, ...), custom_call_target="tpu_custom_call" | custom-call | flops 10000000000 | bytes 1 | tf_op jit(solution)/shard_map/attend_back/pallas_call | solution.py:219
  171.6 10.0 %attend_back.5.refs_2_.refs_3_ = bf16[3,1024,256]{2,1,0:T(8,128)(2,1)S(1)} custom-call(f32[8,384,256]{2,1,0:T(8,128)S(1)} %copy-done.35, bf16[128,1024]{1,0:T(8,128)(2,1)S(1)} %copy-done.64, bf16[1024,128]{1,0:T(8,128)(2,1)S(1)} %copy-done.66, bf16[1024,768]{1,0:T(8,128)(2,1)S(1)} %copy-done.39, bf16[1024,768]{1,0:T(8,128)(2,1)S(1)} %copy-done.41, ...), custom_call_target="tpu_custom_call" | custom-call | flops 10000000000 | bytes 1 | tf_op jit(solution)/shard_map/attend_back/pallas_call | solution.py:219
  182.5 1.8 collective-permute-done.14.come
  184.5 1.7 collective-permute-start.17
  186.2 5.5 %patch_back.1 = bf16[1024,768]{1,0:T(8,128)(2,1)S(1)} custom-call(bf16[3,1024,256]{2,1,0:T(8,128)(2,1)S(1)} %attend_back.3.refs_0_.refs_1_, bf16[3,1024,256]{2,1,0:T(8,128)(2,1)S(1)} %attend_back.4.refs_1_.refs_2_, bf16[3,1024,256]{2,1,0:T(8,128)(2,1)S(1)} %attend_back.5.refs_2_.refs_3_, bf16[1024,768]{1,0:T(8,128)(2,1)S(1)} %copy-done.37, ...), custom_call_target="tpu_custom_call" | custom-call | flops 10000000000 | bytes 1 | tf_op jit(solution)/shard_map/patch_back/pallas_call | solution.py:463
  191.8 2.3 weight_grad.4
  194.3 2.4 weight_grad.5
  197.2 2.3 weight_grad.6.near
  201.0 2.4 weight_grad.7.near
  203.7 1.6 collective-permute-start.20
  205.3 4.7 %collective-permute-done.17.come = bf16[48,6144]{1,0:T(8,128)(2,1)S(1)} collective-permute-done((bf16[48,6144]{1,0:T(8,128)(2,1)S(1)}, bf16[48,6144]{1,0:T(8,128)(2,1)S(1)}, u32[]{:S(2)}, u32[]{:S(2)}) %collective-permute-start.17) | collective-permute-done | bytes 589856 | tf_op jit(solution)/shard_map/ppermute | solution.py:726
  210.3 4.9 %collective-permute-done.16.come = bf16[2,96,1536]{2,1,0:T(8,128)(2,1)S(1)} collective-permute-done((bf16[2,96,1536]{2,1,0:T(8,128)(2,1)S(1)}, bf16[2,96,1536]{2,1,0:T(8,128)(2,1)S(1)}, u32[]{:S(2)}, u32[]{:S(2)}) %collective-permute-start.16) | collective-permute-done | bytes 589856 | tf_op jit(solution)/shard_map/ppermute | solution.py:726
  215.3 3.4 %collective-permute-done.20.come = bf16[2,96,1536]{2,1,0:T(8,128)(2,1)S(1)} collective-permute-done((bf16[2,96,1536]{2,1,0:T(8,128)(2,1)S(1)}, bf16[2,96,1536]{2,1,0:T(8,128)(2,1)S(1)}, u32[]{:S(2)}, u32[]{:S(2)}) %collective-permute-start.20) | collective-permute-done | bytes 589856 | tf_op jit(solution)/shard_map/ppermute | solution.py:726
  221.1 5.7 %collective-permute-done.21.refs_3_ = bf16[1,96,1536]{2,1,0:T(8,128)(2,1)S(1)} collective-permute-done((bf16[1,96,1536]{2,1,0:T(8,128)(2,1)S(1)}, bf16[1,96,1536]{2,1,0:T(8,128)(2,1)S(1)}, u32[]{:S(2)}, u32[]{:S(2)}) %collective-permute-start.21) | collective-permute-done | bytes 294944 | tf_op jit(solution)/shard_map/ppermute | solution.py:726
  228.9 1.4 collective-permute-start.25
  230.3 1.7 collective-permute-start.22
  232.0 5.0 %collective-permute-done.22.come = bf16[48,3072]{1,0:T(8,128)(2,1)S(1)} collective-permute-done((bf16[48,3072]{1,0:T(8,128)(2,1)S(1)}, bf16[48,3072]{1,0:T(8,128)(2,1)S(1)}, u32[]{:S(2)}, u32[]{:S(2)}) %collective-permute-start.22) | collective-permute-done | bytes 294944 | tf_op jit(solution)/shard_map/ppermute | solution.py:726
  237.1 3.5 %collective-permute-done.26.come = bf16[1,96,3072]{2,1,0:T(8,128)(2,1)S(1)} collective-permute-done((bf16[1,96,3072]{2,1,0:T(8,128)(2,1)S(1)}, bf16[1,96,3072]{2,1,0:T(8,128)(2,1)S(1)}, u32[]{:S(2)}, u32[]{:S(2)}) %collective-permute-start.26) | collective-permute-done | bytes 589856 | tf_op jit(solution)/shard_map/ppermute | solution.py:726
  242.5 1.4 collective-permute-start.30
  243.9 1.6 collective-permute-start.24
  245.4 10.8 %collective-permute-done.24.come = bf16[48,3072]{1,0:T(8,128)(2,1)S(1)} collective-permute-done((bf16[48,3072]{1,0:T(8,128)(2,1)S(1)}, bf16[48,3072]{1,0:T(8,128)(2,1)S(1)}, u32[]{:S(2)}, u32[]{:S(2)}) %collective-permute-start.24) | collective-permute-done | bytes 294944 | tf_op jit(solution)/shard_map/ppermute | solution.py:726
  256.5 7.4 %collective-permute-done.27.come = bf16[48,3072]{1,0:T(8,128)(2,1)S(1)} collective-permute-done((bf16[48,3072]{1,0:T(8,128)(2,1)S(1)}, bf16[48,3072]{1,0:T(8,128)(2,1)S(1)}, u32[]{:S(2)}, u32[]{:S(2)}) %collective-permute-start.27) | collective-permute-done | bytes 294944 | tf_op jit(solution)/shard_map/ppermute | solution.py:726
  264.0 2.0 collective-permute-done.31.two_come
  268.4 1.7 collective-permute-start.33
  271.3 2.8 collective-permute-start.29
  274.1 2.5 collective-permute-done.34.come
  276.6 1.8 collective-permute-start.35
  278.4 1.3 collective-permute-start.36
  279.7 6.8 %assemble.2 = (f32[768,2048]{1,0:T(8,128)}, f32[768,2048]{1,0:T(8,128)}, f32[768,128]{1,0:T(8,128)S(1)}) custom-call(s32[3]{0:T(128)S(1)} %get-tuple-element.539.place_ref, bf16[4,96,6144]{2,1,0:T(8,128)(2,1)S(1)} %join_both.2.near_ref, bf16[4,96,6144]{2,1,0:T(8,128)(2,1)S(1)} %collective-permute-done.32.far_ref, bf16[768,2048]{1,0:T(8,128)(2,1)S(1)} %copy-done.10, ...), custom_call_target="tpu_custom_call" | custom-call | flops 10000000000 | bytes 1 | tf_op jit(solution)/shard_map/assemble/pallas_call | solution.py:500
  286.5 2.8 collective-permute-done.28.refs_1_
  289.2 2.2 collective-permute-done.29.refs_2_
  291.5 1.7 collective-permute-done.36.two_come
  293.4 3.3 %collective-permute-start.37 = (bf16[256,768]{1,0:T(8,128)(2,1)S(1)}, bf16[256,768]{1,0:T(8,128)(2,1)S(1)}, u32[]{:S(2)}, u32[]{:S(2)}) collective-permute-start(bf16[256,768]{1,0:T(8,128)(2,1)S(1)} %get-tuple-element.616), channel_id=1, source_target_pairs={{0,3},{1,2},{2,1},{3,0},{4,7},{5,6},{6,5},{7,4},{8,11},{9,10},{10,... | collective-permute-start | bytes 1179656 | tf_op jit(solution)/shard_map/ppermute | solution.py:726
  297.5 6.0 %assemble_turned.1 = f32[2048,768]{1,0:T(8,128)} custom-call(s32[3]{0:T(128)S(1)} %get-tuple-element.539.place_ref, bf16[4,96,6144]{2,1,0:T(8,128)(2,1)S(1)} %join_both.2.near_ref, bf16[4,96,6144]{2,1,0:T(8,128)(2,1)S(1)} %collective-permute-done.32.far_ref), custom_call_target="tpu_custom_call" | custom-call | flops 10000000000 | bytes 1 | tf_op jit(solution)/shard_map/assemble_turned/pallas_call | solution.py:538
  303.5 6.0 %assemble.3 = (f32[768,768]{1,0:T(8,128)}, f32[768,768]{1,0:T(8,128)}, f32[768,768]{1,0:T(8,128)}, f32[768,768]{1,0:T(8,128)}, f32[768,128]{1,0:T(8,128)S(1)}) custom-call(s32[3]{0:T(128)S(1)} %get-tuple-element.539.place_ref, bf16[4,96,3072]{2,1,0:T(8,128)(2,1)S(1)} %join_both.3.near_ref, bf16[4,96,3072]{2,1,0:T(8,128)(2,1)S(1)} %collective-permute-done.38.far_ref, ...), custom_call_target="tpu_custom_call" | custom-call | flops 10000000000 | bytes 1 | tf_op jit(solution)/shard_map/assemble/pallas_call | solution.py:500
  (243 shorter events, 53.5 us)
Async XLA Ops:
  0.6 18.0 %copy-start = (s32[4,128]{1,0:T(4,128)S(1)}, s32[4,128]{1,0:T(4,128)}, u32[]{:S(2)}) copy-start(s32[4,128]{1,0:T(4,128)} %param.27) | copy-start | bytes 6148
  3.2 11.3 %copy-start.23 = (bf16[256,768]{1,0:T(8,128)(2,1)}, bf16[256,768]{1,0:T(8,128)(2,1)S(1)}, u32[]{:S(2)}) copy-start(bf16[256,768]{1,0:T(8,128)(2,1)S(1)} %get-tuple-element.377.piece.refs_0_) | copy-start | bytes 1179652
  3.2 25.0 %collective-permute-start = (bf16[256,768]{1,0:T(8,128)(2,1)}, bf16[256,768]{1,0:T(8,128)(2,1)}, u32[]{:S(2)}, u32[]{:S(2)}) collective-permute-start(bf16[256,768]{1,0:T(8,128)(2,1)} %get-tuple-element.323), channel_id=1, source_target_pairs={{0,1},{1,0},{2,3},{3,2},{4,5},{5,4},{6,7},{7,6},{8,9},{9,8},{10,11... | collective-permute-start | bytes 1179656 | tf_op jit(solution)/shard_map/ppermute | solution.py:726
  6.2 28.7 %collective-permute-start.1 = (bf16[256,768]{1,0:T(8,128)(2,1)}, bf16[256,768]{1,0:T(8,128)(2,1)}, u32[]{:S(2)}, u32[]{:S(2)}) collective-permute-start(bf16[256,768]{1,0:T(8,128)(2,1)} %get-tuple-element.324), channel_id=1, source_target_pairs={{0,2},{1,3},{2,0},{3,1},{4,6},{5,7},{6,4},{7,5},{8,10},{9,11},{10,... | collective-permute-start | bytes 1179656 | tf_op jit(solution)/shard_map/ppermute | solution.py:726
  9.5 36.9 %copy-start.6 = (f32[1,768]{1,0:T(1,128)}, f32[1,768]{1,0:T(1,128)S(1)}, u32[]{:S(2)}) copy-start(f32[1,768]{1,0:T(1,128)S(1)} %broadcast_in_dim.12.gain.refs_16_.refs_5_) | copy-start | bytes 9220
  17.5 19.9 %collective-permute-start.2 = (bf16[256,768]{1,0:T(8,128)(2,1)}, bf16[256,768]{1,0:T(8,128)(2,1)}, u32[]{:S(2)}, u32[]{:S(2)}) collective-permute-start(bf16[256,768]{1,0:T(8,128)(2,1)} %get-tuple-element.335), channel_id=1, source_target_pairs={{0,3},{1,2},{2,1},{3,0},{4,7},{5,6},{6,5},{7,4},{8,11},{9,10},{10,... | collective-permute-start | bytes 1179656 | tf_op jit(solution)/shard_map/ppermute | solution.py:726
  34.8 11.5 %copy-start.24 = (bf16[256,768]{1,0:T(8,128)(2,1)S(1)}, bf16[256,768]{1,0:T(8,128)(2,1)}, u32[]{:S(2)}) copy-start(bf16[256,768]{1,0:T(8,128)(2,1)} %copy-done.23) | copy-start | bytes 1179652
  34.8 11.5 %copy-start.55 = (bf16[256,768]{1,0:T(8,128)(2,1)S(1)}, bf16[256,768]{1,0:T(8,128)(2,1)}, u32[]{:S(2)}) copy-start(bf16[256,768]{1,0:T(8,128)(2,1)} %copy-done.54) | copy-start | bytes 1179652
  34.8 11.5 %copy-start.57 = (bf16[256,768]{1,0:T(8,128)(2,1)S(1)}, bf16[256,768]{1,0:T(8,128)(2,1)}, u32[]{:S(2)}) copy-start(bf16[256,768]{1,0:T(8,128)(2,1)} %copy-done.56) | copy-start | bytes 1179652
  34.8 11.5 %copy-start.59 = (bf16[256,768]{1,0:T(8,128)(2,1)S(1)}, bf16[256,768]{1,0:T(8,128)(2,1)}, u32[]{:S(2)}) copy-start(bf16[256,768]{1,0:T(8,128)(2,1)} %copy-done.58) | copy-start | bytes 1179652
  34.8 11.5 %copy-start.61 = (bf16[256,768]{1,0:T(8,128)(2,1)S(1)}, bf16[256,768]{1,0:T(8,128)(2,1)}, u32[]{:S(2)}) copy-start(bf16[256,768]{1,0:T(8,128)(2,1)} %copy-done.60) | copy-start | bytes 1179652
  37.4 13.0 %copy-start.34 = (f32[8,384,256]{2,1,0:T(8,128)S(1)}, f32[8,384,256]{2,1,0:T(8,128)}, u32[]{:S(2)}) copy-start(f32[8,384,256]{2,1,0:T(8,128)} %copy-done.33) | copy-start | bytes 9437188
  37.4 13.0 %copy-start.63 = (bf16[128,1024]{1,0:T(8,128)(2,1)S(1)}, bf16[128,1024]{1,0:T(8,128)(2,1)}, u32[]{:S(2)}) copy-start(bf16[128,1024]{1,0:T(8,128)(2,1)} %copy-done.62) | copy-start | bytes 786436
  37.4 44.3 %collective-permute-start.3 = (bf16[256,768]{1,0:T(8,128)(2,1)S(1)}, bf16[256,768]{1,0:T(8,128)(2,1)S(1)}, u32[]{:S(2)}, u32[]{:S(2)}) collective-permute-start(bf16[256,768]{1,0:T(8,128)(2,1)S(1)} %get-tuple-element.374), channel_id=1, source_target_pairs={{0,1},{1,0},{2,3},{3,2},{4,5},{5,4},{6,7},{7,6},{8,9},{9,8},{10,11... | collective-permute-start | bytes 1179656 | tf_op jit(solution)/shard_map/ppermute | solution.py:726
  43.9 37.9 %collective-permute-start.4 = (bf16[256,768]{1,0:T(8,128)(2,1)S(1)}, bf16[256,768]{1,0:T(8,128)(2,1)S(1)}, u32[]{:S(2)}, u32[]{:S(2)}) collective-permute-start(bf16[256,768]{1,0:T(8,128)(2,1)S(1)} %get-tuple-element.375), channel_id=1, source_target_pairs={{0,2},{1,3},{2,0},{3,1},{4,6},{5,7},{6,4},{7,5},{8,10},{9,11},{10,... | collective-permute-start | bytes 1179656 | tf_op jit(solution)/shard_map/ppermute | solution.py:726
  44.9 36.8 %collective-permute-start.5 = (bf16[256,768]{1,0:T(8,128)(2,1)S(1)}, bf16[256,768]{1,0:T(8,128)(2,1)S(1)}, u32[]{:S(2)}, u32[]{:S(2)}) collective-permute-start(bf16[256,768]{1,0:T(8,128)(2,1)S(1)} %get-tuple-element.376), channel_id=1, source_target_pairs={{0,3},{1,2},{2,1},{3,0},{4,7},{5,6},{6,5},{7,4},{8,11},{9,10},{10,... | collective-permute-start | bytes 1179656 | tf_op jit(solution)/shard_map/ppermute | solution.py:726
  50.4 20.2 %copy-start.38 = (bf16[1024,768]{1,0:T(8,128)(2,1)}, bf16[1024,768]{1,0:T(8,128)(2,1)S(1)}, u32[]{:S(2)}) copy-start(bf16[1024,768]{1,0:T(8,128)(2,1)S(1)} %get-tuple-element.503.q_ref) | copy-start | bytes 4718596
  50.4 20.2 %copy-start.40 = (bf16[1024,768]{1,0:T(8,128)(2,1)}, bf16[1024,768]{1,0:T(8,128)(2,1)S(1)}, u32[]{:S(2)}) copy-start(bf16[1024,768]{1,0:T(8,128)(2,1)S(1)} %get-tuple-element.504.k_ref) | copy-start | bytes 4718596
  50.4 20.2 %copy-start.42 = (bf16[1024,768]{1,0:T(8,128)(2,1)}, bf16[1024,768]{1,0:T(8,128)(2,1)S(1)}, u32[]{:S(2)}) copy-start(bf16[1024,768]{1,0:T(8,128)(2,1)S(1)} %get-tuple-element.505.v_ref) | copy-start | bytes 4718596
  50.4 20.2 %copy-start.36 = (bf16[1024,768]{1,0:T(8,128)(2,1)}, bf16[1024,768]{1,0:T(8,128)(2,1)S(1)}, u32[]{:S(2)}) copy-start(bf16[1024,768]{1,0:T(8,128)(2,1)S(1)} %get-tuple-element.514.x_ref.refs_3_) | copy-start | bytes 4718596
  50.4 20.2 %copy-start.13 = (bf16[768,768]{1,0:T(8,128)(2,1)S(1)}, bf16[768,768]{1,0:T(8,128)(2,1)}, u32[]{:S(2)}) copy-start(bf16[768,768]{1,0:T(8,128)(2,1)} %in_ref.6) | copy-start | bytes 3538948
  112.0 8.3 %collective-permute-start.6 = (bf16[3,4,96,2048]{3,2,1,0:T(8,128)(2,1)}, bf16[3,4,96,2048]{3,2,1,0:T(8,128)(2,1)}, u32[]{:S(2)}, u32[]{:S(2)}) collective-permute-start(bf16[3,4,96,2048]{3,2,1,0:T(8,128)(2,1)} %get-tuple-element.436), channel_id=1, source_target_pairs={{0,4},{4,0},{8,12},{12,8},{16,20},{20,16},{24,28},{28,24},{1,5},{5... | collective-permute-start | bytes 14155784 | tf_op jit(solution)/shard_map/ppermute | solution.py:726
  112.1 8.1 %copy-start.31 = (bf16[3,4,96,2048]{3,2,1,0:T(8,128)(2,1)S(1)}, bf16[3,4,96,2048]{3,2,1,0:T(8,128)(2,1)}, u32[]{:S(2)}) copy-start(bf16[3,4,96,2048]{3,2,1,0:T(8,128)(2,1)} %get-tuple-element.445.near) | copy-start | bytes 14155780
  120.2 12.4 %copy-start.30 = (bf16[2048,768]{1,0:T(8,128)(2,1)S(1)}, bf16[2048,768]{1,0:T(8,128)(2,1)}, u32[]{:S(2)}) copy-start(bf16[2048,768]{1,0:T(8,128)(2,1)} %copy-done.29) | copy-start | bytes 9437188
  120.2 12.4 %copy-start.73 = (bf16[1024,2048]{1,0:T(8,128)(2,1)S(1)}, bf16[1024,2048]{1,0:T(8,128)(2,1)}, u32[]{:S(2)}) copy-start(bf16[1024,2048]{1,0:T(8,128)(2,1)} %get-tuple-element.455) | copy-start | bytes 12582916
  125.2 31.1 %collective-permute-start.11 = (bf16[2,96,3072]{2,1,0:T(8,128)(2,1)S(1)}, bf16[2,96,3072]{2,1,0:T(8,128)(2,1)S(1)}, u32[]{:S(2)}, u32[]{:S(2)}) collective-permute-start(bf16[2,96,3072]{2,1,0:T(8,128)(2,1)S(1)} %get-tuple-element.448), channel_id=1, source_target_pairs={{0,8},{4,12},{8,0},{12,4},{16,24},{20,28},{24,16},{28,20},{1,9},{5... | collective-permute-start | bytes 3538952 | tf_op jit(solution)/shard_map/ppermute | solution.py:726
  126.7 30.4 %collective-permute-start.10 = (bf16[2,96,3072]{2,1,0:T(8,128)(2,1)S(1)}, bf16[2,96,3072]{2,1,0:T(8,128)(2,1)S(1)}, u32[]{:S(2)}, u32[]{:S(2)}) collective-permute-start(bf16[2,96,3072]{2,1,0:T(8,128)(2,1)S(1)} %get-tuple-element.450), channel_id=1, source_target_pairs={{0,16},{4,20},{8,24},{12,28},{16,0},{20,4},{24,8},{28,12},{1,17},{... | collective-permute-start | bytes 3538952 | tf_op jit(solution)/shard_map/ppermute | solution.py:726
  128.2 7.8 %copy-start.28 = (bf16[2048,768]{1,0:T(8,128)(2,1)S(1)}, bf16[2048,768]{1,0:T(8,128)(2,1)}, u32[]{:S(2)}) copy-start(bf16[2048,768]{1,0:T(8,128)(2,1)} %copy-done.27) | copy-start | bytes 9437188
  128.2 7.8 %copy-start.72 = (bf16[1024,2048]{1,0:T(8,128)(2,1)S(1)}, bf16[1024,2048]{1,0:T(8,128)(2,1)}, u32[]{:S(2)}) copy-start(bf16[1024,2048]{1,0:T(8,128)(2,1)} %get-tuple-element.457) | copy-start | bytes 12582916
  128.2 39.6 %collective-permute-start.7 = (bf16[256,768]{1,0:T(8,128)(2,1)S(1)}, bf16[256,768]{1,0:T(8,128)(2,1)S(1)}, u32[]{:S(2)}, u32[]{:S(2)}) collective-permute-start(bf16[256,768]{1,0:T(8,128)(2,1)S(1)} %get-tuple-element.452), channel_id=1, source_target_pairs={{0,1},{1,0},{2,3},{3,2},{4,5},{5,4},{6,7},{7,6},{8,9},{9,8},{10,11... | collective-permute-start | bytes 1179656 | tf_op jit(solution)/shard_map/ppermute | solution.py:726
  129.3 38.6 %collective-permute-start.8 = (bf16[256,768]{1,0:T(8,128)(2,1)S(1)}, bf16[256,768]{1,0:T(8,128)(2,1)S(1)}, u32[]{:S(2)}, u32[]{:S(2)}) collective-permute-start(bf16[256,768]{1,0:T(8,128)(2,1)S(1)} %get-tuple-element.453), channel_id=1, source_target_pairs={{0,2},{1,3},{2,0},{3,1},{4,6},{5,7},{6,4},{7,5},{8,10},{9,11},{10,... | collective-permute-start | bytes 1179656 | tf_op jit(solution)/shard_map/ppermute | solution.py:726
  131.2 36.6 %collective-permute-start.9 = (bf16[256,768]{1,0:T(8,128)(2,1)S(1)}, bf16[256,768]{1,0:T(8,128)(2,1)S(1)}, u32[]{:S(2)}, u32[]{:S(2)}) collective-permute-start(bf16[256,768]{1,0:T(8,128)(2,1)S(1)} %get-tuple-element.454), channel_id=1, source_target_pairs={{0,3},{1,2},{2,1},{3,0},{4,7},{5,6},{6,5},{7,4},{8,11},{9,10},{10,... | collective-permute-start | bytes 1179656 | tf_op jit(solution)/shard_map/ppermute | solution.py:726
  156.5 14.6 %collective-permute-start.12 = (bf16[1,96,3072]{2,1,0:T(8,128)(2,1)S(1)}, bf16[1,96,3072]{2,1,0:T(8,128)(2,1)S(1)}, u32[]{:S(2)}, u32[]{:S(2)}) collective-permute-start(bf16[1,96,3072]{2,1,0:T(8,128)(2,1)S(1)} %get-tuple-element.476), channel_id=1, source_target_pairs={{0,16},{4,20},{8,24},{12,28},{16,0},{20,4},{24,8},{28,12},{1,17},{... | collective-permute-start | bytes 1769480 | tf_op jit(solution)/shard_map/ppermute | solution.py:726
  157.4 13.7 %collective-permute-start.13 = (bf16[1,96,3072]{2,1,0:T(8,128)(2,1)S(1)}, bf16[1,96,3072]{2,1,0:T(8,128)(2,1)S(1)}, u32[]{:S(2)}, u32[]{:S(2)}) collective-permute-start(bf16[1,96,3072]{2,1,0:T(8,128)(2,1)S(1)} %get-tuple-element.480), channel_id=1, source_target_pairs={{0,8},{4,12},{8,0},{12,4},{16,24},{20,28},{24,16},{28,20},{1,9},{5... | collective-permute-start | bytes 1769480 | tf_op jit(solution)/shard_map/ppermute | solution.py:726
  171.4 12.9 %collective-permute-start.14 = (bf16[48,6144]{1,0:T(8,128)(2,1)S(1)}, bf16[48,6144]{1,0:T(8,128)(2,1)S(1)}, u32[]{:S(2)}, u32[]{:S(2)}) collective-permute-start(bf16[48,6144]{1,0:T(8,128)(2,1)S(1)} %get-tuple-element.499), channel_id=1, source_target_pairs={{0,1},{1,0},{2,3},{3,2},{4,5},{5,4},{6,7},{7,6},{8,9},{9,8},{10,11... | collective-permute-start | bytes 1769480 | tf_op jit(solution)/shard_map/ppermute | solution.py:726
  171.6 10.1 %copy-start.51 = (bf16[1024,768]{1,0:T(8,128)(2,1)S(1)}, bf16[1024,768]{1,0:T(8,128)(2,1)}, u32[]{:S(2)}) copy-start(bf16[1024,768]{1,0:T(8,128)(2,1)} %copy-done.50) | copy-start | bytes 4718596
  184.5 25.6 %collective-permute-start.17 = (bf16[48,6144]{1,0:T(8,128)(2,1)S(1)}, bf16[48,6144]{1,0:T(8,128)(2,1)S(1)}, u32[]{:S(2)}, u32[]{:S(2)}) collective-permute-start(bf16[48,6144]{1,0:T(8,128)(2,1)S(1)} %add_up.4.near), channel_id=1, source_target_pairs={{0,2},{1,3},{2,0},{3,1},{4,6},{5,7},{6,4},{7,5},{8,10},{9,11},{10,... | collective-permute-start | bytes 1769480 | tf_op jit(solution)/shard_map/ppermute | solution.py:726
  194.2 5.4 %collective-permute-start.15 = (bf16[4,96,1536]{2,1,0:T(8,128)(2,1)S(1)}, bf16[4,96,1536]{2,1,0:T(8,128)(2,1)S(1)}, u32[]{:S(2)}, u32[]{:S(2)}) collective-permute-start(bf16[4,96,1536]{2,1,0:T(8,128)(2,1)S(1)} %weight_grad.4), channel_id=1, source_target_pairs={{0,4},{4,0},{8,12},{12,8},{16,20},{20,16},{24,28},{28,24},{1,5},{5... | collective-permute-start | bytes 3538952 | tf_op jit(solution)/shard_map/ppermute | solution.py:726
  196.7 6.8 %collective-permute-start.18 = (bf16[4,96,1536]{2,1,0:T(8,128)(2,1)S(1)}, bf16[4,96,1536]{2,1,0:T(8,128)(2,1)S(1)}, u32[]{:S(2)}, u32[]{:S(2)}) collective-permute-start(bf16[4,96,1536]{2,1,0:T(8,128)(2,1)S(1)} %weight_grad.5), channel_id=1, source_target_pairs={{0,4},{4,0},{8,12},{12,8},{16,20},{20,16},{24,28},{28,24},{1,5},{5... | collective-permute-start | bytes 3538952 | tf_op jit(solution)/shard_map/ppermute | solution.py:726
  199.9 15.3 %collective-permute-start.16 = (bf16[2,96,1536]{2,1,0:T(8,128)(2,1)S(1)}, bf16[2,96,1536]{2,1,0:T(8,128)(2,1)S(1)}, u32[]{:S(2)}, u32[]{:S(2)}) collective-permute-start(bf16[2,96,1536]{2,1,0:T(8,128)(2,1)S(1)} %get-tuple-element.549), channel_id=1, source_target_pairs={{0,8},{4,12},{8,0},{12,4},{16,24},{20,28},{24,16},{28,20},{1,9},{5... | collective-permute-start | bytes 1769480 | tf_op jit(solution)/shard_map/ppermute | solution.py:726
  203.7 15.0 %collective-permute-start.20 = (bf16[2,96,1536]{2,1,0:T(8,128)(2,1)S(1)}, bf16[2,96,1536]{2,1,0:T(8,128)(2,1)S(1)}, u32[]{:S(2)}, u32[]{:S(2)}) collective-permute-start(bf16[2,96,1536]{2,1,0:T(8,128)(2,1)S(1)} %get-tuple-element.560), channel_id=1, source_target_pairs={{0,16},{4,20},{8,24},{12,28},{16,0},{20,4},{24,8},{28,12},{1,17},{... | collective-permute-start | bytes 1769480 | tf_op jit(solution)/shard_map/ppermute | solution.py:726
  210.2 17.3 %collective-permute-start.23 = (bf16[48,6144]{1,0:T(8,128)(2,1)S(1)}, bf16[48,6144]{1,0:T(8,128)(2,1)S(1)}, u32[]{:S(2)}, u32[]{:S(2)}) collective-permute-start(bf16[48,6144]{1,0:T(8,128)(2,1)S(1)} %add_up.5.near), channel_id=1, source_target_pairs={{0,1},{1,0},{2,3},{3,2},{4,5},{5,4},{6,7},{7,6},{8,9},{9,8},{10,11... | collective-permute-start | bytes 1769480 | tf_op jit(solution)/shard_map/ppermute | solution.py:726
  218.9 7.8 %collective-permute-start.21 = (bf16[1,96,1536]{2,1,0:T(8,128)(2,1)S(1)}, bf16[1,96,1536]{2,1,0:T(8,128)(2,1)S(1)}, u32[]{:S(2)}, u32[]{:S(2)}) collective-permute-start(bf16[1,96,1536]{2,1,0:T(8,128)(2,1)S(1)} %get-tuple-element.570), channel_id=1, source_target_pairs={{0,8},{4,12},{8,0},{12,4},{16,24},{20,28},{24,16},{28,20},{1,9},{5... | collective-permute-start | bytes 884744 | tf_op jit(solution)/shard_map/ppermute | solution.py:726
  219.9 7.5 %collective-permute-start.19 = (bf16[1,96,1536]{2,1,0:T(8,128)(2,1)S(1)}, bf16[1,96,1536]{2,1,0:T(8,128)(2,1)S(1)}, u32[]{:S(2)}, u32[]{:S(2)}) collective-permute-start(bf16[1,96,1536]{2,1,0:T(8,128)(2,1)S(1)} %get-tuple-element.566), channel_id=1, source_target_pairs={{0,16},{4,20},{8,24},{12,28},{16,0},{20,4},{24,8},{28,12},{1,17},{... | collective-permute-start | bytes 884744 | tf_op jit(solution)/shard_map/ppermute | solution.py:726
  227.6 13.0 %collective-permute-start.26 = (bf16[1,96,3072]{2,1,0:T(8,128)(2,1)S(1)}, bf16[1,96,3072]{2,1,0:T(8,128)(2,1)S(1)}, u32[]{:S(2)}, u32[]{:S(2)}) collective-permute-start(bf16[1,96,3072]{2,1,0:T(8,128)(2,1)S(1)} %get-tuple-element.583.near), channel_id=1, source_target_pairs={{0,16},{4,20},{8,24},{12,28},{16,0},{20,4},{24,8},{28,12},{1,17},{... | collective-permute-start | bytes 1769480 | tf_op jit(solution)/shard_map/ppermute | solution.py:726
  228.9 12.7 %collective-permute-start.25 = (bf16[1,96,3072]{2,1,0:T(8,128)(2,1)S(1)}, bf16[1,96,3072]{2,1,0:T(8,128)(2,1)S(1)}, u32[]{:S(2)}, u32[]{:S(2)}) collective-permute-start(bf16[1,96,3072]{2,1,0:T(8,128)(2,1)S(1)} %get-tuple-element.585.near), channel_id=1, source_target_pairs={{0,8},{4,12},{8,0},{12,4},{16,24},{20,28},{24,16},{28,20},{1,9},{5... | collective-permute-start | bytes 1769480 | tf_op jit(solution)/shard_map/ppermute | solution.py:726
  230.3 6.7 %collective-permute-start.22 = (bf16[48,3072]{1,0:T(8,128)(2,1)S(1)}, bf16[48,3072]{1,0:T(8,128)(2,1)S(1)}, u32[]{:S(2)}, u32[]{:S(2)}) collective-permute-start(bf16[48,3072]{1,0:T(8,128)(2,1)S(1)} %get-tuple-element.576), channel_id=1, source_target_pairs={{0,1},{1,0},{2,3},{3,2},{4,5},{5,4},{6,7},{7,6},{8,9},{9,8},{10,11... | collective-permute-start | bytes 884744 | tf_op jit(solution)/shard_map/ppermute | solution.py:726
  241.7 24.3 %collective-permute-start.31 = (bf16[2,96,3072]{2,1,0:T(8,128)(2,1)S(1)}, bf16[2,96,3072]{2,1,0:T(8,128)(2,1)S(1)}, u32[]{:S(2)}, u32[]{:S(2)}) collective-permute-start(bf16[2,96,3072]{2,1,0:T(8,128)(2,1)S(1)} %join.5.two), channel_id=1, source_target_pairs={{0,16},{4,20},{8,24},{12,28},{16,0},{20,4},{24,8},{28,12},{1,17},{... | collective-permute-start | bytes 3538952 | tf_op jit(solution)/shard_map/ppermute | solution.py:726
  242.5 24.3 %collective-permute-start.30 = (bf16[2,96,3072]{2,1,0:T(8,128)(2,1)S(1)}, bf16[2,96,3072]{2,1,0:T(8,128)(2,1)S(1)}, u32[]{:S(2)}, u32[]{:S(2)}) collective-permute-start(bf16[2,96,3072]{2,1,0:T(8,128)(2,1)S(1)} %join.4.one), channel_id=1, source_target_pairs={{0,8},{4,12},{8,0},{12,4},{16,24},{20,28},{24,16},{28,20},{1,9},{5... | collective-permute-start | bytes 3538952 | tf_op jit(solution)/shard_map/ppermute | solution.py:726
  243.9 12.4 %collective-permute-start.24 = (bf16[48,3072]{1,0:T(8,128)(2,1)S(1)}, bf16[48,3072]{1,0:T(8,128)(2,1)S(1)}, u32[]{:S(2)}, u32[]{:S(2)}) collective-permute-start(bf16[48,3072]{1,0:T(8,128)(2,1)S(1)} %add_up.6.near), channel_id=1, source_target_pairs={{0,2},{1,3},{2,0},{3,1},{4,6},{5,7},{6,4},{7,5},{8,10},{9,11},{10,... | collective-permute-start | bytes 884744 | tf_op jit(solution)/shard_map/ppermute | solution.py:726
  256.4 7.5 %collective-permute-start.27 = (bf16[48,3072]{1,0:T(8,128)(2,1)S(1)}, bf16[48,3072]{1,0:T(8,128)(2,1)S(1)}, u32[]{:S(2)}, u32[]{:S(2)}) collective-permute-start(bf16[48,3072]{1,0:T(8,128)(2,1)S(1)} %add_up.7.near), channel_id=1, source_target_pairs={{0,1},{1,0},{2,3},{3,2},{4,5},{5,4},{6,7},{7,6},{8,9},{9,8},{10,11... | collective-permute-start | bytes 884744 | tf_op jit(solution)/shard_map/ppermute | solution.py:726
  263.9 15.8 %copy-start.10 = (bf16[768,2048]{1,0:T(8,128)(2,1)S(1)}, bf16[768,2048]{1,0:T(8,128)(2,1)}, u32[]{:S(2)}) copy-start(bf16[768,2048]{1,0:T(8,128)(2,1)} %refs_0_.3) | copy-start | bytes 9437188
  264.0 15.8 %copy-start.12 = (bf16[768,2048]{1,0:T(8,128)(2,1)S(1)}, bf16[768,2048]{1,0:T(8,128)(2,1)}, u32[]{:S(2)}) copy-start(bf16[768,2048]{1,0:T(8,128)(2,1)} %refs_1_.3) | copy-start | bytes 9437188
  267.1 12.7 %collective-permute-start.32 = (bf16[4,96,6144]{2,1,0:T(8,128)(2,1)S(1)}, bf16[4,96,6144]{2,1,0:T(8,128)(2,1)S(1)}, u32[]{:S(2)}, u32[]{:S(2)}) collective-permute-start(bf16[4,96,6144]{2,1,0:T(8,128)(2,1)S(1)} %join_both.2.near_ref), channel_id=1, source_target_pairs={{0,4},{4,0},{8,12},{12,8},{16,20},{20,16},{24,28},{28,24},{1,5},{5... | collective-permute-start | bytes 14155784 | tf_op jit(solution)/shard_map/ppermute | solution.py:726
  267.1 9.4 %collective-permute-start.34 = (bf16[1,96,1536]{2,1,0:T(8,128)(2,1)S(1)}, bf16[1,96,1536]{2,1,0:T(8,128)(2,1)S(1)}, u32[]{:S(2)}, u32[]{:S(2)}) collective-permute-start(bf16[1,96,1536]{2,1,0:T(8,128)(2,1)S(1)} %get-tuple-element.599.near), channel_id=1, source_target_pairs={{0,16},{4,20},{8,24},{12,28},{16,0},{20,4},{24,8},{28,12},{1,17},{... | collective-permute-start | bytes 884744 | tf_op jit(solution)/shard_map/ppermute | solution.py:726
  268.4 10.0 %collective-permute-start.33 = (bf16[1,96,1536]{2,1,0:T(8,128)(2,1)S(1)}, bf16[1,96,1536]{2,1,0:T(8,128)(2,1)S(1)}, u32[]{:S(2)}, u32[]{:S(2)}) collective-permute-start(bf16[1,96,1536]{2,1,0:T(8,128)(2,1)S(1)} %get-tuple-element.601.near), channel_id=1, source_target_pairs={{0,8},{4,12},{8,0},{12,4},{16,24},{20,28},{24,16},{28,20},{1,9},{5... | collective-permute-start | bytes 884744 | tf_op jit(solution)/shard_map/ppermute | solution.py:726
  270.1 19.1 %collective-permute-start.28 = (bf16[256,768]{1,0:T(8,128)(2,1)S(1)}, bf16[256,768]{1,0:T(8,128)(2,1)S(1)}, u32[]{:S(2)}, u32[]{:S(2)}) collective-permute-start(bf16[256,768]{1,0:T(8,128)(2,1)S(1)} %get-tuple-element.593), channel_id=1, source_target_pairs={{0,1},{1,0},{2,3},{3,2},{4,5},{5,4},{6,7},{7,6},{8,9},{9,8},{10,11... | collective-permute-start | bytes 1179656 | tf_op jit(solution)/shard_map/ppermute | solution.py:726
  271.3 20.1 %collective-permute-start.29 = (bf16[256,768]{1,0:T(8,128)(2,1)S(1)}, bf16[256,768]{1,0:T(8,128)(2,1)S(1)}, u32[]{:S(2)}, u32[]{:S(2)}) collective-permute-start(bf16[256,768]{1,0:T(8,128)(2,1)S(1)} %get-tuple-element.594), channel_id=1, source_target_pairs={{0,2},{1,3},{2,0},{3,1},{4,6},{5,7},{6,4},{7,5},{8,10},{9,11},{10,... | collective-permute-start | bytes 1179656 | tf_op jit(solution)/shard_map/ppermute | solution.py:726
  276.6 16.5 %collective-permute-start.35 = (bf16[2,96,1536]{2,1,0:T(8,128)(2,1)S(1)}, bf16[2,96,1536]{2,1,0:T(8,128)(2,1)S(1)}, u32[]{:S(2)}, u32[]{:S(2)}) collective-permute-start(bf16[2,96,1536]{2,1,0:T(8,128)(2,1)S(1)} %join.6.one), channel_id=1, source_target_pairs={{0,8},{4,12},{8,0},{12,4},{16,24},{20,28},{24,16},{28,20},{1,9},{5... | collective-permute-start | bytes 1769480 | tf_op jit(solution)/shard_map/ppermute | solution.py:726
  278.4 14.7 %collective-permute-start.36 = (bf16[2,96,1536]{2,1,0:T(8,128)(2,1)S(1)}, bf16[2,96,1536]{2,1,0:T(8,128)(2,1)S(1)}, u32[]{:S(2)}, u32[]{:S(2)}) collective-permute-start(bf16[2,96,1536]{2,1,0:T(8,128)(2,1)S(1)} %join.7.two), channel_id=1, source_target_pairs={{0,16},{4,20},{8,24},{12,28},{16,0},{20,4},{24,8},{28,12},{1,17},{... | collective-permute-start | bytes 1769480 | tf_op jit(solution)/shard_map/ppermute | solution.py:726
  293.3 10.2 %collective-permute-start.38 = (bf16[4,96,3072]{2,1,0:T(8,128)(2,1)S(1)}, bf16[4,96,3072]{2,1,0:T(8,128)(2,1)S(1)}, u32[]{:S(2)}, u32[]{:S(2)}) collective-permute-start(bf16[4,96,3072]{2,1,0:T(8,128)(2,1)S(1)} %join_both.3.near_ref), channel_id=1, source_target_pairs={{0,4},{4,0},{8,12},{12,8},{16,20},{20,16},{24,28},{28,24},{1,5},{5... | collective-permute-start | bytes 7077896 | tf_op jit(solution)/shard_map/ppermute | solution.py:726
  293.4 16.3 %collective-permute-start.37 = (bf16[256,768]{1,0:T(8,128)(2,1)S(1)}, bf16[256,768]{1,0:T(8,128)(2,1)S(1)}, u32[]{:S(2)}, u32[]{:S(2)}) collective-permute-start(bf16[256,768]{1,0:T(8,128)(2,1)S(1)} %get-tuple-element.616), channel_id=1, source_target_pairs={{0,3},{1,2},{2,1},{3,0},{4,7},{5,6},{6,5},{7,4},{8,11},{9,10},{10,... | collective-permute-start | bytes 1179656 | tf_op jit(solution)/shard_map/ppermute | solution.py:726
  303.4 6.2 %copy-start.69 = (f32[768]{0:T(1024)S(1)}, f32[768]{0:T(1024)}, u32[]{:S(2)}) copy-start(f32[768]{0:T(1024)} %param.15) | copy-start | bytes 9220
  303.5 8.0 %copy-start.1 = (s32[4,128]{1,0:T(4,128)S(1)}, s32[4,128]{1,0:T(4,128)}, u32[]{:S(2)}) copy-start(s32[4,128]{1,0:T(4,128)} %param.27) | copy-start | bytes 6148
  (49 other events, 124.3 us)
